TPU v7x, 256 devices: a whole 4x4x8 slice. The times are simulated.
256 devices in a mesh: expert: 64 (over z, y, core), seq: 4 (over x).
Axes of the slice: x: 4, y: 4, z: 8, core: 2. Of those that a mesh axis runs over, the one named last changes fastest.
Arguments:
- routes: int32 [32768, 10], P(('expert', 'seq')), may hold values from 0 to 63, all different within a row; in each aligned block of 128 rows (0 to 127, 128 to 255, ...) at most 30 rows name the same one
- combine_weights: float32 [32768, 10], P(('expert', 'seq')), may hold values from 0.02 to 0.5
- expert_rows: bfloat16 [64, 4, 64, 30, 1024], P('expert', 'seq'), may hold values from -6 to 6
- expert_weight: bfloat16 [64, 1024, 2048], P('expert'), may hold values from -0.1875 to 0.1875
- conv_grad: bfloat16 [32768, 4096], P(('expert', 'seq')), may hold values from -6 to 6
- conv_input: bfloat16 [32768, 4096], P(('expert', 'seq')), may hold values from -6 to 6
- conv_weight: float32 [4, 4096], P(None, 'seq'), may hold values from -2.5 to 2.5
Outputs:
- token_grad: bfloat16 [32768, 2048], P(('expert', 'seq'))
- input_grad: bfloat16 [32768, 4096], P('expert', 'seq')
- weight_grad: float32 [4, 4096], P(None, 'seq')
Inputs may be any that keep to these rules, and one draw needn't show every extreme that they name: `routes`: each row names 10 different experts. In each aligned block of 128 rows (the tokens of one device) no expert is named by more than 30 rows, a bound that some block reaches.
All inputs are finite; a program needn't handle non-finite values.
Results may differ from a plain program's by a relative error of at most 0.0049.
Values may be sent and summed in bfloat16 or wider, within the bound.
No kernel may reach another device: no remote copies, remote signals or barrier semaphores. Data moves between devices by JAX's collectives and lax.ppermute only.
A program may use at most 128 MiB of HBM per device.

v0:
```python
import functools
import math

import jax
import jax.numpy as jnp
from jax import lax
from jax.experimental import pallas as pl
from jax.experimental.pallas import tpu as pltpu
from jax.sharding import PartitionSpec as P

NZ, NY, NC = 8, 4, 2
WIDTHS = (1024, 1024)
OVERLAP = 2
PACKED = {1152: 384, 896: 896, 1280: 640, 768: 384, 1024: 512}
BF = jnp.bfloat16
F32 = jnp.float32
VMEM = 40 * 1024 * 1024
LARGE = 58 * 1024 * 1024
QUICK = pl.CostEstimate(flops=0, bytes_accessed=0, transcendentals=0)


def device_at(z, y, c):
    return (z * NY + y) * NC + c


def shift(value, dz=0, dy=0, dc=0):
    pairs = [
        (device_at(z, y, c), device_at((z + dz) % NZ, (y + dy) % NY, (c + dc) % NC))
        for z in range(NZ)
        for y in range(NY)
        for c in range(NC)
    ]
    return lax.ppermute(value, "expert", pairs)


def after(value, *first):
    return lax.optimization_barrier((value, *first))[0]


def from_behind(value, axis, steps):
    count = lax.axis_size(axis)
    leading, last = (max(0, -steps), min(count, count - steps))
    return lax.ppermute(value, axis, [(source, source + steps) for source in range(leading, last)])


def conv_kernel(grad_ref, input_ref, taps_ref, result_ref, sums_ref):
    count, reach = result_ref.shape[0], taps_ref.shape[0] - 1
    inputs = input_ref[...].astype(F32)
    near = [inputs[offset : offset + count + reach] for offset in range(reach + 1)]
    taps = [taps_ref[offset : offset + 1] for offset in range(reach + 1)]
    pre_act = taps[0] * near[0]
    for offset in range(1, reach + 1):
        pre_act = pre_act + taps[offset] * near[offset]
    sigmoid = 1.0 / (1.0 + jnp.exp(-pre_act))
    pre_grad = grad_ref[...].astype(F32) * sigmoid * (1.0 + pre_act * (1.0 - sigmoid))
    result = taps[0] * pre_grad[reach : reach + count]
    for offset in range(1, reach + 1):
        result = result + taps[offset] * pre_grad[reach - offset : reach - offset + count]
    result_ref[...] = result.astype(BF)
    here = pre_grad[:count]
    sums = [jnp.sum(here * near[o][:count], axis=0, keepdims=True) for o in range(reach + 1)]
    sums_ref[...] = jnp.concatenate(sums, axis=0)


def conv_core(grad_rows, input_rows, input_past, grad_next, input_next, kernel):
    count, channels = grad_rows.shape
    taps = kernel.shape[0]
    tile = 256
    input_ext = jnp.concatenate([input_past, input_rows, input_next], axis=0)
    grad_ext = jnp.concatenate([grad_rows, grad_next], axis=0)
    column = lambda i: (0, i)
    return pl.pallas_call(
        conv_kernel,
        grid=(channels // tile,),
        in_specs=[
            pl.BlockSpec((grad_ext.shape[0], tile), column),
            pl.BlockSpec((input_ext.shape[0], tile), column),
            pl.BlockSpec((taps, tile), column),
        ],
        out_specs=[pl.BlockSpec((count, tile), column), pl.BlockSpec((taps, tile), column)],
        out_shape=[
            jax.ShapeDtypeStruct((count, channels), BF),
            jax.ShapeDtypeStruct((taps, channels), F32),
        ],
        compiler_params=pltpu.CompilerParams(vmem_limit_bytes=VMEM),
        cost_estimate=QUICK,
        name="conv",
    )(grad_ext, input_ext, kernel)


def conv_edges(conv_grad, conv_input, conv_weight):
    reach = conv_weight.shape[0] - 1
    with jax.named_scope("convedges"):
        input_past = from_behind(conv_input[-reach:], ("expert", "seq"), 1)
        front = jnp.stack([conv_grad[:reach], conv_input[:reach]], axis=0)
        front_next = from_behind(front, ("expert", "seq"), -1)
    with jax.named_scope("convtaps"):
        count = lax.axis_size("seq")
        kernel = jnp.broadcast_to(conv_weight[None], (count, *conv_weight.shape))
        kernel = lax.all_to_all(kernel, "seq", split_axis=0, concat_axis=0, tiled=True)
        kernel = jnp.concatenate([kernel[i] for i in range(count)], axis=1)
    return input_past, front_next, kernel


def conv_local(conv_grad, conv_input, edges):
    input_past, front_next, kernel = edges
    with jax.named_scope("convcore"):
        return conv_core(conv_grad, conv_input, input_past, front_next[0], front_next[1], kernel)


def conv_rest(result, taps):
    count = lax.axis_size("seq")
    width = taps.shape[1] // count
    with jax.named_scope("convmove"):
        result = lax.all_to_all(result, "seq", split_axis=1, concat_axis=0, tiled=True)
    with jax.named_scope("tapsmove"):
        taps = jnp.stack([taps[:, i * width : (i + 1) * width] for i in range(count)])
        taps = lax.all_to_all(taps, "seq", split_axis=0, concat_axis=0, tiled=True)
        return result, jnp.sum(taps, axis=0)


PARTNERS = (
    lambda z, y, c: (z, y, c ^ 1),
    lambda z, y, c: (z ^ 1, y, c),
    lambda z, y, c: (z ^ 2, y, c),
    lambda z, y, c: (z ^ 4, y, c),
    lambda z, y, c: (z, y ^ 1, c),
    lambda z, y, c: (z, y ^ 2, c),
)


def flip_sum(value, partner):
    pairs = [
        (device_at(z, y, c), device_at(*partner(z, y, c)))
        for z in range(NZ)
        for y in range(NY)
        for c in range(NC)
    ]
    return value + lax.ppermute(value, "expert", pairs)


def sort_kernel(order_ref, rows_ref, out_ref):
    order = order_ref[...]
    parts = out_ref.shape[0]
    for group in range(rows_ref.shape[0]):
        moved = jnp.dot(order, rows_ref[group], preferred_element_type=F32).astype(BF)
        out_ref[:, group] = moved.reshape(parts, moved.shape[0] // parts, moved.shape[1])


def sort_rows(rows, y, c):
    capacity, groups, depth = rows.shape
    parts = NY * NC
    size = 2 * groups
    count = capacity // 2
    rows = rows.reshape(count, size, depth)
    place = lax.broadcasted_iota(jnp.int32, (size, size), 0)
    source = lax.broadcasted_iota(jnp.int32, (size, size), 1)
    part, inner = place // (2 * NZ), place % (2 * NZ)
    core, row = (c + part // NY) % NC, (y + part % NY) % NY
    wanted = (inner // NZ) * groups + (inner % NZ) * parts + row * NC + core
    order = (source == wanted).astype(BF)
    step = 5 if count % 5 == 0 else 1
    out = pl.pallas_call(
        sort_kernel,
        grid=(count // step,),
        in_specs=[
            pl.BlockSpec((size, size), lambda i: (0, 0)),
            pl.BlockSpec((step, size, depth), lambda i: (i, 0, 0)),
        ],
        out_specs=pl.BlockSpec((parts, step, size // parts, depth), lambda i: (0, i, 0, 0)),
        out_shape=jax.ShapeDtypeStruct((parts, count, size // parts, depth), BF),
        compiler_params=pltpu.CompilerParams(vmem_limit_bytes=VMEM),
        cost_estimate=QUICK,
        name="sort",
    )(order, rows)
    return out.reshape(parts * count * (size // parts), depth)


def turned(info, experts):
    top, tokens = info.shape[0] // 2, info.shape[1]
    named, gates = info[:top], info[top:]
    rows, marks = [], []
    for expert in experts:
        hit = named == expert.astype(F32)
        rows.append(jnp.sum(jnp.where(hit, gates, 0.0), axis=0, keepdims=True))
        marks.append(jnp.sum(jnp.where(hit, 1.0, 0.0), axis=0, keepdims=True))
    gate, mark = jnp.concatenate(rows, axis=0), jnp.concatenate(marks, axis=0)
    down = lax.broadcasted_iota(jnp.int32, (tokens, tokens), 0)
    along = lax.broadcasted_iota(jnp.int32, (tokens, tokens), 1)
    same = jnp.where(down == along, 1.0, 0.0).astype(BF)
    before = jnp.where(along < down, 1.0, 0.0).astype(BF)

    def turn(matrix, value):
        return lax.dot_general(
            matrix, value, (((1,), (1,)), ((), ())), preferred_element_type=F32
        )

    return turn(same, gate.astype(BF)), turn(before, mark.astype(BF))


def put_gates(out_ref, at, lanes, columns, picks, lane_slot):
    gate, slot = columns

    def chosen(value):
        result = value[:, picks[-1] : picks[-1] + 1]
        for lane, pick in reversed(list(zip(lanes, picks[:-1], strict=True))):
            result = jnp.where(lane, value[:, pick : pick + 1], result)
        return result

    here = chosen(slot) == lane_slot
    out_ref[at] = jnp.where(here, chosen(gate), 0.0).astype(BF)


def own_lanes(pair, goal):
    lane = lax.broadcasted_iota(jnp.int32, (1, pair), 1)
    first = lane < pair // NC
    inner = jnp.where(first, lane, lane - pair // NC)
    return first, jnp.where(inner % NZ == goal, inner // NZ, -1).astype(F32)


def position(me):
    return me // (NY * NC), (me // NC) % NY, me % NC


def column_kernel(order, me_ref, info_ref, out_ref):
    sources, _, pair = out_ref.shape
    tokens = info_ref.shape[2]
    z, y, c = position(me_ref[0])
    experts = [
        device_at(z, (y + NY - behind) % NY, (c + core) % NC)
        for behind in ROWS_FROM
        for core in range(NC)
    ]
    for number, place in enumerate(order):
        columns = turned(info_ref[place], experts)
        first, lane_slot = own_lanes(pair, (z + place) % NZ)
        for source in range(sources):
            picks = (NC * source, NC * source + 1)
            at = (source, slice(number * tokens, (number + 1) * tokens), slice(None))
            put_gates(out_ref, at, [first], columns, picks, lane_slot)


def column_matrix(me, info, order, capacity):
    tokens = info.shape[2]
    sources, pair = len(ROWS_FROM), NC * capacity * NZ
    return pl.pallas_call(
        functools.partial(column_kernel, order),
        grid_spec=pltpu.PrefetchScalarGridSpec(
            num_scalar_prefetch=1,
            grid=(1,),
            in_specs=[pl.BlockSpec(info.shape, lambda i, p: (0, 0, 0))],
            out_specs=pl.BlockSpec((sources, len(order) * tokens, pair), lambda i, p: (0, 0, 0)),
        ),
        out_shape=jax.ShapeDtypeStruct((sources, len(order) * tokens, pair), BF),
        compiler_params=pltpu.CompilerParams(vmem_limit_bytes=VMEM),
        cost_estimate=QUICK,
        name="gatescolumn",
    )(me.reshape(1), info)


def multiply_kernel(rows_ref, weight_ref, out_ref):
    out_ref[...] = jnp.dot(rows_ref[...], weight_ref[0], preferred_element_type=F32).astype(BF)


def multiply_half(rows, weight, half, start, columns):
    size, depth = rows.shape[0] // 2, rows.shape[1]
    tile = 256 if start % 256 == 0 and columns % 256 == 0 else 128
    return pl.pallas_call(
        multiply_kernel,
        grid=(columns // tile,),
        in_specs=[
            pl.BlockSpec((size, depth), lambda i: (half, 0)),
            pl.BlockSpec((1, depth, tile), lambda i: (0, 0, start // tile + i)),
        ],
        out_specs=pl.BlockSpec((size, tile), lambda i: (0, i)),
        out_shape=jax.ShapeDtypeStruct((size, columns), BF),
        compiler_params=pltpu.CompilerParams(vmem_limit_bytes=LARGE),
        cost_estimate=QUICK,
        name="multiply",
    )(rows, weight)


def pack_kernel(kept_ref, other_ref, *out_refs):
    block = out_refs[0].shape[0] // NC
    for part, ref in enumerate(out_refs):
        ref[:block] = kept_ref[part * block : (part + 1) * block]
        ref[block:] = other_ref[part * block : (part + 1) * block]


def pack(kept, other):
    size, columns = kept.shape
    tile, pair = PACKED[columns], NC * size // NY
    return pl.pallas_call(
        pack_kernel,
        grid=(columns // tile,),
        in_specs=[pl.BlockSpec((size, tile), lambda i: (0, i))] * 2,
        out_specs=[pl.BlockSpec((pair, tile), lambda i: (0, i))] * NY,
        out_shape=[jax.ShapeDtypeStruct((pair, columns), BF)] * NY,
        compiler_params=pltpu.CompilerParams(vmem_limit_bytes=VMEM),
        cost_estimate=QUICK,
        name="pack",
    )(kept, other)


def merge_kernel(matrix_ref, *refs):
    rows, out_ref = refs[:-1], refs[-1]
    total = None
    for part, ref in enumerate(rows):
        term = jnp.dot(matrix_ref[part], ref[...], preferred_element_type=F32)
        total = term if total is None else total + term
    out_ref[...] = total.astype(out_ref.dtype)


def merge_rows(matrix, rows, dtype, steps):
    sources, places, depth = matrix.shape
    columns = rows[0].shape[1]
    step = places // steps
    return pl.pallas_call(
        merge_kernel,
        grid=(steps,),
        in_specs=[pl.BlockSpec((sources, step, depth), lambda i: (0, i, 0))]
        + [pl.BlockSpec((depth, columns), lambda i: (0, 0))] * sources,
        out_specs=pl.BlockSpec((step, columns), lambda i: (i, 0)),
        out_shape=jax.ShapeDtypeStruct((places, columns), dtype),
        compiler_params=pltpu.CompilerParams(vmem_limit_bytes=LARGE if steps > 1 else VMEM),
        cost_estimate=QUICK,
        name="merge",
    )(matrix, *rows)


def z_ring(four, rest, gate):
    half = four.shape[1] // 2
    ahead = shift(four[:, :half], dz=1)
    back = shift(four[:, half:], dz=-1)
    zeros = jnp.zeros_like(ahead)
    ahead = jnp.concatenate([ahead, zeros], axis=1)
    back = jnp.concatenate([zeros, back], axis=1)

    def part(apart):
        return rest[ORDER.index(apart)]

    for apart in (3, 2, 1):
        ahead, back = gate(4 - apart, ahead, back)
        ahead = shift((part(apart) + ahead.astype(F32)).astype(BF), dz=1)
        back = shift((part(NZ - apart) + back.astype(F32)).astype(BF), dz=-1)
    return (part(0) + ahead.astype(F32) + back.astype(F32)).astype(BF)


ROWS_FROM = (0, 1, 3, 2)
ORDER = (3, 5, 2, 6, 1, 7, 0)
BEHIND = (0, -1, 1, -2, 2)


def expert_part(
    routes,
    combine_weights,
    expert_rows,
    expert_weight,
    conv_grad,
    conv_input,
    conv_weight,
    tokens_total,
):
    me = lax.axis_index("expert")
    z, y, c = me // (NY * NC), (me // NC) % NY, me % NC
    capacity = expert_rows.shape[3]
    tokens, top = routes.shape
    block = capacity * NZ
    half = NY * block

    with jax.named_scope("sort"):
        rows = jnp.transpose(expert_rows[0, 0], (1, 0, 2))
        rows = sort_rows(rows, y, c)

    starts = [sum(WIDTHS[:chunk]) for chunk in range(len(WIDTHS))]
    def ready(chunk, rows_now):
        place = (starts[chunk], WIDTHS[chunk])
        weight = expert_weight[0, :, place[0] : sum(place)]
        with jax.named_scope(f"multiply{chunk}"):
            if chunk:
                out = multiply_half(rows_now, expert_weight, 1, *place)
                kept = multiply_half(after(rows_now, out), expert_weight, 0, *place)
            else:
                out = jnp.dot(rows_now[half:], weight, preferred_element_type=F32).astype(BF)
                kept = after(rows_now, out)[:half]
                kept = jnp.dot(kept, weight, preferred_element_type=F32).astype(BF)
        with jax.named_scope(f"swap{chunk}"):
            other = shift(out, dc=1)
        with jax.named_scope(f"pack{chunk}"):
            return pack(kept, other), out

    with jax.named_scope("info"):
        column = jnp.concatenate([routes.T.astype(F32), combine_weights.T], axis=0)[None]
        column = after(column, rows)
        column = jnp.concatenate([column, shift(column, dz=-1)], axis=0)

    def exchange(chunk, parts):
        with jax.named_scope(f"rows{chunk}"):
            return [parts[0]] + [shift(parts[apart], dy=apart) for apart in ROWS_FROM[1:]]

    count = len(WIDTHS)
    parts_first, out = ready(0, rows)
    parts = [parts_first]
    arrived = [exchange(0, parts[0])]
    begin = parts[0][1:]
    edges = conv_edges(
        after(conv_grad, *begin), after(conv_input, *begin), after(conv_weight, rows)
    )
    with jax.named_scope("info"):
        column = after(column, *parts[0][1:])
        for apart in (2, 4):
            column = jnp.concatenate([column, shift(column, dz=-apart)], axis=0)
    with jax.named_scope("gatescolumn"):
        matrix_four = column_matrix(me, column, (4,), capacity)
        matrix_rest = column_matrix(me, column, ORDER, capacity)
    result, taps = conv_local(conv_grad, conv_input, edges)
    for chunk in range(1, count):
        parts.append(ready(chunk, after(rows, *parts[-1][1:]))[0])
        waited = [*arrived[chunk - 1][1:], matrix_rest, result, taps]
        arrived.append(exchange(chunk, [after(part, *waited) for part in parts[chunk]]))
    input_grad, taps = conv_rest(after(result, *arrived[0][1:]), after(taps, *arrived[0][1:]))

    results, progress = [], [None] * count
    for chunk in range(count):
        slots_now = arrived[chunk]
        last = chunk + 1 == count
        if not last:
            slots_now = [after(value, *parts[chunk + 1][1:]) for value in slots_now]
        if chunk >= 1:
            slots_now = [after(value, progress[chunk - 1]) for value in slots_now]

        def gate(step, ahead, back):
            first = []
            if step == OVERLAP:
                progress[chunk] = ahead
            if not last and step == 2:
                first += [*arrived[chunk + 1][1:], taps_at[1], input_grad]
            return [after(value, *first) for value in (ahead, back)] if first else (ahead, back)

        with jax.named_scope(f"merge{chunk}"):
            four = merge_rows(matrix_four, slots_now, BF, 1)
            slots_now = [after(value, four) for value in slots_now]
            rest = merge_rows(matrix_rest, slots_now, F32, 2)
            rest = rest.reshape(NZ - 1, tokens, WIDTHS[chunk])
        if chunk == 0:
            taps_at = [taps]
            for number, partner in enumerate(PARTNERS):
                with jax.named_scope(f"taps{number}"):
                    taps_at.append(flip_sum(taps_at[-1], partner))
        with jax.named_scope(f"ring{chunk}"):
            results.append(z_ring(four, rest, gate))
    weight_grad = taps_at[-1] * (1.0 / math.sqrt(tokens_total))
    return jnp.concatenate(results, axis=1), input_grad, weight_grad


def local(routes, combine_weights, expert_rows, expert_weight, conv_grad, conv_input, conv_weight):
    tokens_total = routes.shape[0] * lax.axis_size("expert") * lax.axis_size("seq")
    return expert_part(
        routes,
        combine_weights,
        expert_rows,
        expert_weight,
        conv_grad,
        conv_input,
        conv_weight,
        tokens_total,
    )


def solution(mesh):
    placed = (
        P(("expert", "seq"), None),
        P(("expert", "seq"), None),
        P("expert", "seq", None, None, None),
        P("expert", None, None),
        P(("expert", "seq"), None),
        P(("expert", "seq"), None),
        P(None, "seq"),
    )
    return jax.shard_map(
        local,
        mesh=mesh,
        in_specs=placed,
        out_specs=(P(("expert", "seq"), None), P("expert", "seq"), P(None, "seq")),
        check_vma=False,
    )
```

profile of v0, /device:TPU:6, one launch (start us, length us, event | category | flops | bytes accessed | tf_op | source)
XLA Modules:
  0.0 211.4 jit_solution(14911055000422512451)
XLA Ops:
  5.3 3.6 %fusion.7 = bf16[960,1024]{1,0:T(8,128)(2,1)} fusion(bf16[960,1024]{1,0:T(8,128)(2,1)S(1)} %bitcast.60, bf16[1,1024,2048]{2,1,0:T(8,128)(2,1)S(1)} %copy-done.12), kind=kOutput, calls=%fused_computation.7 | convolution fusion | flops 2014248960 | bytes 6029312 | tf_op jit(solution)/shard_map/multiply0/dot_general | solution.py:384
  8.9 5.9 %collective-permute-start = (f32[1,20,128]{2,1,0:T(8,128)S(1)}, f32[1,20,128]{2,1,0:T(8,128)S(1)}, u32[]{:S(2)}, u32[]{:S(2)}) collective-permute-start(f32[1,20,128]{2,1,0:T(8,128)S(1)} %maximum_bitcast_fusion), channel_id=1, source_target_pairs={{0,224},{4,228},{8,232},{12,236},{16,240},{20,244},{24,248},{28,25... | collective-permute-start | bytes 30728 | tf_op jit(solution)/shard_map/info/ppermute | solution.py:33
  15.5 4.8 %all-to-all-start = ((f32[4,4,1024]{2,1,0:T(4,128)}), f32[4,4,1024]{2,1,0:T(4,128)S(1)}, u32[]{:S(2)}, u32[]{:S(2)}) async-start(f32[4,4,1024]{2,1,0:T(4,128)} %broadcast_in_dim.10), calls=%async_computation | async-start | bytes 131072 | tf_op jit(solution)/shard_map/convtaps/all_to_all | solution.py:100
  20.3 5.7 %fusion.10.kept_ref = bf16[960,1024]{1,0:T(8,128)(2,1)} fusion(bf16[1,1024,2048]{2,1,0:T(8,128)(2,1)} %weight_ref.3, bf16[1920,1024]{1,0:T(8,128)(2,1)} %bitcast.54), kind=kOutput, calls=%fused_computation.8 | convolution fusion | flops 2014248960 | bytes 6029312 | tf_op jit(solution)/shard_map/multiply0/dot_general | solution.py:386
  32.5 2.9 %collective-permute-start.7 = (bf16[480,1024]{1,0:T(8,128)(2,1)}, bf16[480,1024]{1,0:T(8,128)(2,1)S(1)}, u32[]{:S(2)}, u32[]{:S(2)}) collective-permute-start(bf16[480,1024]{1,0:T(8,128)(2,1)} %get-tuple-element.48), channel_id=1, source_target_pairs={{0,16},{4,20},{8,24},{12,28},{16,0},{20,4},{24,8},{28,12},{32,48},... | collective-permute-start | bytes 2949128 | tf_op jit(solution)/shard_map/rows0/ppermute | solution.py:33
  38.5 5.9 %multiply.2 = bf16[960,1024]{1,0:T(8,128)(2,1)} custom-call(bf16[1920,1024]{1,0:T(8,128)(2,1)} %bitcast.55, bf16[1,1024,2048]{2,1,0:T(8,128)(2,1)} %weight_ref.3), custom_call_target="tpu_custom_call" | custom-call | tf_op jit(solution)/shard_map/multiply1/multiply/pallas_call | solution.py:268
  45.1 5.9 %multiply.3.kept_ref = bf16[960,1024]{1,0:T(8,128)(2,1)} custom-call(bf16[1920,1024]{1,0:T(8,128)(2,1)} %bitcast.56, bf16[1,1024,2048]{2,1,0:T(8,128)(2,1)} %weight_ref.3), custom_call_target="tpu_custom_call" | custom-call | tf_op jit(solution)/shard_map/multiply1/multiply/pallas_call | solution.py:268
  51.0 2.9 %collective-permute-start.10 = (bf16[2,3,4096]{2,1,0:T(4,128)(2,1)}, bf16[2,3,4096]{2,1,0:T(4,128)(2,1)S(1)}, u32[]{:S(2)}, u32[]{:S(2)}) collective-permute-start(bf16[2,3,4096]{2,1,0:T(4,128)(2,1)} %pad_maximum_fusion.3), channel_id=1, source_target_pairs={{1,0},{2,1},{3,2},{4,3},{5,4},{6,5},{7,6},{8,7},{9,8},{10,9},{11,1... | collective-permute-start | bytes 147464 | tf_op jit(solution)/shard_map/convedges/ppermute | solution.py:43
  53.9 4.2 %collective-permute-done.10 = bf16[2,3,4096]{2,1,0:T(4,128)(2,1)S(1)} collective-permute-done((bf16[2,3,4096]{2,1,0:T(4,128)(2,1)}, bf16[2,3,4096]{2,1,0:T(4,128)(2,1)S(1)}, u32[]{:S(2)}, u32[]{:S(2)}) %collective-permute-start.10) | collective-permute-done | bytes 49184 | tf_op jit(solution)/shard_map/convedges/ppermute | solution.py:43
  64.5 5.1 %conv.1 = (bf16[128,4096]{1,0:T(8,128)(2,1)S(1)}, f32[4,4096]{1,0:T(4,128)S(1)}) custom-call(bf16[131,4096]{1,0:T(8,128)(2,1)S(1)} %pad_maximum_fusion.grad_ref, bf16[134,4096]{1,0:T(8,128)(2,1)S(1)} %pad_maximum_fusion.1.input_ref, f32[4,4096]{1,0:T(4,128)S(1)} %pad_maximum_fusion.4.taps_ref), custom_call_target="tpu_custom_call" | custom-call | tf_op jit(solution)/shard_map/convcore/conv/pallas_call | solution.py:72
  70.6 3.0 %collective-permute-done.3 = f32[4,20,128]{2,1,0:T(8,128)S(1)} collective-permute-done((f32[4,20,128]{2,1,0:T(8,128)S(1)}, f32[4,20,128]{2,1,0:T(8,128)S(1)}, u32[]{:S(2)}, u32[]{:S(2)}) %collective-permute-start.3) | collective-permute-done | bytes 40992 | tf_op jit(solution)/shard_map/info/ppermute | solution.py:33
  78.0 3.9 %pack.3 = (bf16[480,1024]{1,0:T(8,128)(2,1)S(1)}, bf16[480,1024]{1,0:T(8,128)(2,1)}, bf16[480,1024]{1,0:T(8,128)(2,1)}, bf16[480,1024]{1,0:T(8,128)(2,1)}) custom-call(bf16[960,1024]{1,0:T(8,128)(2,1)S(1)} %copy-done.2, bf16[960,1024]{1,0:T(8,128)(2,1)} %collective-permute-done.4.other_ref), custom_call_target="tpu_custom_call" | custom-call | tf_op jit(solution)/shard_map/pack1/pack/pallas_call | solution.py:293
  88.8 8.1 %merge.5 = f32[896,1024]{1,0:T(8,128)} custom-call(bf16[4,896,480]{2,1,0:T(8,128)(2,1)} %copy-done.1, bf16[480,1024]{1,0:T(8,128)(2,1)} %copy-done.4, bf16[480,1024]{1,0:T(8,128)(2,1)} %copy-done.5, bf16[480,1024]{1,0:T(8,128)(2,1)} %copy-done.7, bf16[480,1024]{1,0:T(8,128)(2,1)} %copy-done.6), custom_call_target="tpu_custom_call" | custom-call | tf_op jit(solution)/shard_map/merge0/merge/pallas_call | solution.py:318
  99.8 4.8 %all-to-all-start.1 = ((f32[4,4,1024]{2,1,0:T(4,128)}), f32[4,4,1024]{2,1,0:T(4,128)S(1)}, u32[]{:S(2)}, u32[]{:S(2)}) async-start(f32[4,4,1024]{2,1,0:T(4,128)} %pad_maximum_fusion.5), calls=%async_computation.1 | async-start | bytes 131072 | tf_op jit(solution)/shard_map/tapsmove/all_to_all | solution.py:118
  108.2 6.3 %all-to-all-start.2 = ((bf16[128,4,1024]{2,0,1:T(8,128)(2,1)}), bf16[128,4,1024]{2,0,1:T(8,128)(2,1)}, u32[]{:S(2)}, u32[]{:S(2)}) async-start(bf16[128,4,1024]{2,0,1:T(8,128)(2,1)} %bitcast.59), calls=%async_computation.2 | async-start | bytes 2097152 | tf_op jit(solution)/shard_map/convmove/all_to_all | solution.py:115
  114.4 13.9 %collective-permute-done.14.refs_3_ = bf16[480,1024]{1,0:T(8,128)(2,1)} collective-permute-done((bf16[480,1024]{1,0:T(8,128)(2,1)}, bf16[480,1024]{1,0:T(8,128)(2,1)}, u32[]{:S(2)}, u32[]{:S(2)}) %collective-permute-start.14) | collective-permute-done | bytes 983072 | tf_op jit(solution)/shard_map/rows1/ppermute | solution.py:33
  132.0 10.4 %collective-permute-start.15 = (f32[4,1024]{1,0:T(4,128)S(1)}, f32[4,1024]{1,0:T(4,128)S(1)}, u32[]{:S(2)}, u32[]{:S(2)}) collective-permute-start(f32[4,1024]{1,0:T(4,128)S(1)} %reduce_sum.9), channel_id=1, source_target_pairs={{0,4},{4,0},{8,12},{12,8},{16,20},{20,16},{24,28},{28,24},{32,36},... | collective-permute-start | bytes 49160 | tf_op jit(solution)/shard_map/taps0/ppermute | solution.py:139
  142.4 8.0 %merge.7 = f32[896,1024]{1,0:T(8,128)} custom-call(bf16[4,896,480]{2,1,0:T(8,128)(2,1)} %copy-done.1, bf16[480,1024]{1,0:T(8,128)(2,1)} %copy-done.8, bf16[480,1024]{1,0:T(8,128)(2,1)} %collective-permute-done.12.refs_1_, bf16[480,1024]{1,0:T(8,128)(2,1)} %collective-permute-done.13.refs_2_, bf16[480,1024]{1,0:T(8,128)(2,1)} %collective-permute-done.14.refs_3_), custom_call_target="tpu_custom_call" | custom-call | tf_op jit(solution)/shard_map/merge1/merge/pallas_call | solution.py:318
  156.1 3.5 %collective-permute-done.30 = f32[4,1024]{1,0:T(4,128)S(1)} collective-permute-done((f32[4,1024]{1,0:T(4,128)S(1)}, f32[4,1024]{1,0:T(4,128)S(1)}, u32[]{:S(2)}, u32[]{:S(2)}) %collective-permute-start.30) | collective-permute-done | bytes 16416 | tf_op jit(solution)/shard_map/taps1/ppermute | solution.py:139
  165.7 3.2 %collective-permute-start.32 = (f32[4,1024]{1,0:T(4,128)S(1)}, f32[4,1024]{1,0:T(4,128)S(1)}, u32[]{:S(2)}, u32[]{:S(2)}) collective-permute-start(f32[4,1024]{1,0:T(4,128)S(1)} %add.162), channel_id=1, source_target_pairs={{0,128},{4,132},{8,136},{12,140},{16,144},{20,148},{24,152},{28,15... | collective-permute-start | bytes 49160 | tf_op jit(solution)/shard_map/taps3/ppermute | solution.py:139
  168.8 2.8 %collective-permute-start.26 = (bf16[128,512]{1,0:T(8,128)(2,1)S(1)}, bf16[128,512]{1,0:T(8,128)(2,1)S(1)}, u32[]{:S(2)}, u32[]{:S(2)}) collective-permute-start(bf16[128,512]{1,0:T(8,128)(2,1)S(1)} %get-tuple-element.96), channel_id=1, source_target_pairs={{0,224},{4,228},{8,232},{12,236},{16,240},{20,244},{24,248},{28,25... | collective-permute-start | bytes 393224 | tf_op jit(solution)/shard_map/ring1/ppermute | solution.py:33
  175.6 3.8 %collective-permute-start.27 = (bf16[128,1024]{1,0:T(8,128)(2,1)S(1)}, bf16[128,1024]{1,0:T(8,128)(2,1)S(1)}, u32[]{:S(2)}, u32[]{:S(2)}) collective-permute-start(bf16[128,1024]{1,0:T(8,128)(2,1)S(1)} %get-tuple-element.90), channel_id=1, source_target_pairs={{0,224},{4,228},{8,232},{12,236},{16,240},{20,244},{24,248},{28,25... | collective-permute-start | bytes 786440 | tf_op jit(solution)/shard_map/ring1/ppermute | solution.py:33
  194.6 3.1 %collective-permute-start.21 = (bf16[128,1024]{1,0:T(8,128)(2,1)S(1)}, bf16[128,1024]{1,0:T(8,128)(2,1)S(1)}, u32[]{:S(2)}, u32[]{:S(2)}) collective-permute-start(bf16[128,1024]{1,0:T(8,128)(2,1)S(1)} %fusion.25), channel_id=1, source_target_pairs={{0,224},{4,228},{8,232},{12,236},{16,240},{20,244},{24,248},{28,25... | collective-permute-start | bytes 786440 | tf_op jit(solution)/shard_map/ring0/ppermute | solution.py:33
  199.2 3.1 %collective-permute-start.29 = (bf16[128,1024]{1,0:T(8,128)(2,1)S(1)}, bf16[128,1024]{1,0:T(8,128)(2,1)S(1)}, u32[]{:S(2)}, u32[]{:S(2)}) collective-permute-start(bf16[128,1024]{1,0:T(8,128)(2,1)S(1)} %fusion.17), channel_id=1, source_target_pairs={{0,224},{4,228},{8,232},{12,236},{16,240},{20,244},{24,248},{28,25... | collective-permute-start | bytes 786440 | tf_op jit(solution)/shard_map/ring1/ppermute | solution.py:33
  (151 shorter events, 85.2 us)
Async XLA Ops:
  8.9 17.2 %collective-permute-start.1 = (bf16[960,1024]{1,0:T(8,128)(2,1)}, bf16[960,1024]{1,0:T(8,128)(2,1)S(1)}, u32[]{:S(2)}, u32[]{:S(2)}) collective-permute-start(bf16[960,1024]{1,0:T(8,128)(2,1)} %fusion.7), channel_id=1, source_target_pairs={{0,4},{4,0},{8,12},{12,8},{16,20},{20,16},{24,28},{28,24},{32,36},... | collective-permute-start | bytes 5898248 | tf_op jit(solution)/shard_map/swap0/ppermute | solution.py:33
  8.9 17.1 %collective-permute-start = (f32[1,20,128]{2,1,0:T(8,128)S(1)}, f32[1,20,128]{2,1,0:T(8,128)S(1)}, u32[]{:S(2)}, u32[]{:S(2)}) collective-permute-start(f32[1,20,128]{2,1,0:T(8,128)S(1)} %maximum_bitcast_fusion), channel_id=1, source_target_pairs={{0,224},{4,228},{8,232},{12,236},{16,240},{20,244},{24,248},{28,25... | collective-permute-start | bytes 30728 | tf_op jit(solution)/shard_map/info/ppermute | solution.py:33
  15.5 10.5 %all-to-all-start = ((f32[4,4,1024]{2,1,0:T(4,128)}), f32[4,4,1024]{2,1,0:T(4,128)S(1)}, u32[]{:S(2)}, u32[]{:S(2)}) async-start(f32[4,4,1024]{2,1,0:T(4,128)} %broadcast_in_dim.10), calls=%async_computation | async-start | bytes 131072 | tf_op jit(solution)/shard_map/convtaps/all_to_all | solution.py:100
  29.5 21.5 %collective-permute-start.2 = (f32[2,20,128]{2,1,0:T(8,128)S(1)}, f32[2,20,128]{2,1,0:T(8,128)S(1)}, u32[]{:S(2)}, u32[]{:S(2)}) collective-permute-start(f32[2,20,128]{2,1,0:T(8,128)S(1)} %pad_maximum_fusion.7), channel_id=1, source_target_pairs={{0,192},{4,196},{8,200},{12,204},{16,208},{20,212},{24,216},{28,22... | collective-permute-start | bytes 61448 | tf_op jit(solution)/shard_map/info/ppermute | solution.py:33
  30.9 47.0 %collective-permute-start.5 = (bf16[480,1024]{1,0:T(8,128)(2,1)}, bf16[480,1024]{1,0:T(8,128)(2,1)S(1)}, u32[]{:S(2)}, u32[]{:S(2)}) collective-permute-start(bf16[480,1024]{1,0:T(8,128)(2,1)} %get-tuple-element.47), channel_id=1, source_target_pairs={{0,8},{4,12},{8,16},{12,20},{16,24},{20,28},{24,0},{28,4},{32,40},... | collective-permute-start | bytes 2949128 | tf_op jit(solution)/shard_map/rows0/ppermute | solution.py:33
  32.5 45.4 %collective-permute-start.7 = (bf16[480,1024]{1,0:T(8,128)(2,1)}, bf16[480,1024]{1,0:T(8,128)(2,1)S(1)}, u32[]{:S(2)}, u32[]{:S(2)}) collective-permute-start(bf16[480,1024]{1,0:T(8,128)(2,1)} %get-tuple-element.48), channel_id=1, source_target_pairs={{0,16},{4,20},{8,24},{12,28},{16,0},{20,4},{24,8},{28,12},{32,48},... | collective-permute-start | bytes 2949128 | tf_op jit(solution)/shard_map/rows0/ppermute | solution.py:33
  35.4 42.5 %collective-permute-start.6 = (bf16[480,1024]{1,0:T(8,128)(2,1)S(1)}, bf16[480,1024]{1,0:T(8,128)(2,1)S(1)}, u32[]{:S(2)}, u32[]{:S(2)}) collective-permute-start(bf16[480,1024]{1,0:T(8,128)(2,1)S(1)} %get-tuple-element.49), channel_id=1, source_target_pairs={{0,24},{4,28},{8,0},{12,4},{16,8},{20,12},{24,16},{28,20},{32,56},... | collective-permute-start | bytes 2949128 | tf_op jit(solution)/shard_map/rows0/ppermute | solution.py:33
  44.4 33.5 %collective-permute-start.4 = (bf16[960,1024]{1,0:T(8,128)(2,1)}, bf16[960,1024]{1,0:T(8,128)(2,1)}, u32[]{:S(2)}, u32[]{:S(2)}) collective-permute-start(bf16[960,1024]{1,0:T(8,128)(2,1)} %multiply.2), channel_id=1, source_target_pairs={{0,4},{4,0},{8,12},{12,8},{16,20},{20,16},{24,28},{28,24},{32,36},... | collective-permute-start | bytes 5898248 | tf_op jit(solution)/shard_map/swap1/ppermute | solution.py:33
  81.8 46.5 %collective-permute-start.12 = (bf16[480,1024]{1,0:T(8,128)(2,1)}, bf16[480,1024]{1,0:T(8,128)(2,1)}, u32[]{:S(2)}, u32[]{:S(2)}) collective-permute-start(bf16[480,1024]{1,0:T(8,128)(2,1)} %get-tuple-element.70), channel_id=1, source_target_pairs={{0,8},{4,12},{8,16},{12,20},{16,24},{20,28},{24,0},{28,4},{32,40},... | collective-permute-start | bytes 2949128 | tf_op jit(solution)/shard_map/rows1/ppermute | solution.py:33
  82.7 45.6 %collective-permute-start.13 = (bf16[480,1024]{1,0:T(8,128)(2,1)}, bf16[480,1024]{1,0:T(8,128)(2,1)}, u32[]{:S(2)}, u32[]{:S(2)}) collective-permute-start(bf16[480,1024]{1,0:T(8,128)(2,1)} %get-tuple-element.71), channel_id=1, source_target_pairs={{0,24},{4,28},{8,0},{12,4},{16,8},{20,12},{24,16},{28,20},{32,56},... | collective-permute-start | bytes 2949128 | tf_op jit(solution)/shard_map/rows1/ppermute | solution.py:33
  85.1 43.2 %collective-permute-start.14 = (bf16[480,1024]{1,0:T(8,128)(2,1)}, bf16[480,1024]{1,0:T(8,128)(2,1)}, u32[]{:S(2)}, u32[]{:S(2)}) collective-permute-start(bf16[480,1024]{1,0:T(8,128)(2,1)} %get-tuple-element.72), channel_id=1, source_target_pairs={{0,16},{4,20},{8,24},{12,28},{16,0},{20,4},{24,8},{28,12},{32,48},... | collective-permute-start | bytes 2949128 | tf_op jit(solution)/shard_map/rows1/ppermute | solution.py:33
  98.0 16.4 %collective-permute-start.9 = (bf16[128,1024]{1,0:T(8,128)(2,1)S(1)}, bf16[128,1024]{1,0:T(8,128)(2,1)S(1)}, u32[]{:S(2)}, u32[]{:S(2)}) collective-permute-start(bf16[128,1024]{1,0:T(8,128)(2,1)S(1)} %fusion.26), channel_id=1, source_target_pairs={{0,32},{4,36},{8,40},{12,44},{16,48},{20,52},{24,56},{28,60},{32,6... | collective-permute-start | bytes 786440 | tf_op jit(solution)/shard_map/ring0/ppermute | solution.py:33
  108.2 45.2 %all-to-all-start.2 = ((bf16[128,4,1024]{2,0,1:T(8,128)(2,1)}), bf16[128,4,1024]{2,0,1:T(8,128)(2,1)}, u32[]{:S(2)}, u32[]{:S(2)}) async-start(bf16[128,4,1024]{2,0,1:T(8,128)(2,1)} %bitcast.59), calls=%async_computation.2 | async-start | bytes 2097152 | tf_op jit(solution)/shard_map/convmove/all_to_all | solution.py:115
  130.9 19.6 %collective-permute-start.22 = (bf16[128,512]{1,0:T(8,128)(2,1)S(1)}, bf16[128,512]{1,0:T(8,128)(2,1)S(1)}, u32[]{:S(2)}, u32[]{:S(2)}) collective-permute-start(bf16[128,512]{1,0:T(8,128)(2,1)S(1)} %get-tuple-element.95), channel_id=1, source_target_pairs={{0,32},{4,36},{8,40},{12,44},{16,48},{20,52},{24,56},{28,60},{32,6... | collective-permute-start | bytes 393224 | tf_op jit(solution)/shard_map/ring1/ppermute | solution.py:33
  132.0 20.6 %collective-permute-start.15 = (f32[4,1024]{1,0:T(4,128)S(1)}, f32[4,1024]{1,0:T(4,128)S(1)}, u32[]{:S(2)}, u32[]{:S(2)}) collective-permute-start(f32[4,1024]{1,0:T(4,128)S(1)} %reduce_sum.9), channel_id=1, source_target_pairs={{0,4},{4,0},{8,12},{12,8},{16,20},{20,16},{24,28},{28,24},{32,36},... | collective-permute-start | bytes 49160 | tf_op jit(solution)/shard_map/taps0/ppermute | solution.py:139
  151.5 12.9 %collective-permute-start.23 = (bf16[128,1024]{1,0:T(8,128)(2,1)S(1)}, bf16[128,1024]{1,0:T(8,128)(2,1)S(1)}, u32[]{:S(2)}, u32[]{:S(2)}) collective-permute-start(bf16[128,1024]{1,0:T(8,128)(2,1)S(1)} %fusion.18), channel_id=1, source_target_pairs={{0,32},{4,36},{8,40},{12,44},{16,48},{20,52},{24,56},{28,60},{32,6... | collective-permute-start | bytes 786440 | tf_op jit(solution)/shard_map/ring1/ppermute | solution.py:33
  154.7 17.0 %collective-permute-start.16 = (bf16[128,1024]{1,0:T(8,128)(2,1)S(1)}, bf16[128,1024]{1,0:T(8,128)(2,1)S(1)}, u32[]{:S(2)}, u32[]{:S(2)}) collective-permute-start(bf16[128,1024]{1,0:T(8,128)(2,1)S(1)} %fusion.27), channel_id=1, source_target_pairs={{0,32},{4,36},{8,40},{12,44},{16,48},{20,52},{24,56},{28,60},{32,6... | collective-permute-start | bytes 786440 | tf_op jit(solution)/shard_map/ring0/ppermute | solution.py:33
  165.7 13.8 %collective-permute-start.32 = (f32[4,1024]{1,0:T(4,128)S(1)}, f32[4,1024]{1,0:T(4,128)S(1)}, u32[]{:S(2)}, u32[]{:S(2)}) collective-permute-start(f32[4,1024]{1,0:T(4,128)S(1)} %add.162), channel_id=1, source_target_pairs={{0,128},{4,132},{8,136},{12,140},{16,144},{20,148},{24,152},{28,15... | collective-permute-start | bytes 49160 | tf_op jit(solution)/shard_map/taps3/ppermute | solution.py:139
  175.6 12.3 %collective-permute-start.27 = (bf16[128,1024]{1,0:T(8,128)(2,1)S(1)}, bf16[128,1024]{1,0:T(8,128)(2,1)S(1)}, u32[]{:S(2)}, u32[]{:S(2)}) collective-permute-start(bf16[128,1024]{1,0:T(8,128)(2,1)S(1)} %get-tuple-element.90), channel_id=1, source_target_pairs={{0,224},{4,228},{8,232},{12,236},{16,240},{20,244},{24,248},{28,25... | collective-permute-start | bytes 786440 | tf_op jit(solution)/shard_map/ring1/ppermute | solution.py:33
  179.4 11.3 %collective-permute-start.33 = (f32[4,1024]{1,0:T(4,128)S(1)}, f32[4,1024]{1,0:T(4,128)S(1)}, u32[]{:S(2)}, u32[]{:S(2)}) collective-permute-start(f32[4,1024]{1,0:T(4,128)S(1)} %add.163), channel_id=1, source_target_pairs={{0,8},{4,12},{8,0},{12,4},{16,24},{20,28},{24,16},{28,20},{32,40},... | collective-permute-start | bytes 49160 | tf_op jit(solution)/shard_map/taps4/ppermute | solution.py:139
  188.0 11.2 %collective-permute-start.28 = (bf16[128,1024]{1,0:T(8,128)(2,1)S(1)}, bf16[128,1024]{1,0:T(8,128)(2,1)S(1)}, u32[]{:S(2)}, u32[]{:S(2)}) collective-permute-start(bf16[128,1024]{1,0:T(8,128)(2,1)S(1)} %fusion.16), channel_id=1, source_target_pairs={{0,224},{4,228},{8,232},{12,236},{16,240},{20,244},{24,248},{28,25... | collective-permute-start | bytes 786440 | tf_op jit(solution)/shard_map/ring1/ppermute | solution.py:33
  190.7 11.6 %collective-permute-start.34 = (f32[4,1024]{1,0:T(4,128)S(1)}, f32[4,1024]{1,0:T(4,128)S(1)}, u32[]{:S(2)}, u32[]{:S(2)}) collective-permute-start(f32[4,1024]{1,0:T(4,128)S(1)} %add.164), channel_id=1, source_target_pairs={{0,16},{4,20},{8,24},{12,28},{16,0},{20,4},{24,8},{28,12},{32,48},... | collective-permute-start | bytes 49160 | tf_op jit(solution)/shard_map/taps5/ppermute | solution.py:139
  191.7 11.3 %collective-permute-start.17 = (bf16[128,1024]{1,0:T(8,128)(2,1)S(1)}, bf16[128,1024]{1,0:T(8,128)(2,1)S(1)}, u32[]{:S(2)}, u32[]{:S(2)}) collective-permute-start(bf16[128,1024]{1,0:T(8,128)(2,1)S(1)} %get-tuple-element.87), channel_id=1, source_target_pairs={{0,32},{4,36},{8,40},{12,44},{16,48},{20,52},{24,56},{28,60},{32,6... | collective-permute-start | bytes 786440 | tf_op jit(solution)/shard_map/ring0/ppermute | solution.py:33
  191.7 14.3 %collective-permute-start.25 = (bf16[128,1024]{1,0:T(8,128)(2,1)S(1)}, bf16[128,1024]{1,0:T(8,128)(2,1)S(1)}, u32[]{:S(2)}, u32[]{:S(2)}) collective-permute-start(bf16[128,1024]{1,0:T(8,128)(2,1)S(1)} %get-tuple-element.89), channel_id=1, source_target_pairs={{0,32},{4,36},{8,40},{12,44},{16,48},{20,52},{24,56},{28,60},{32,6... | collective-permute-start | bytes 786440 | tf_op jit(solution)/shard_map/ring1/ppermute | solution.py:33
  (33 other events, 366.8 us)
where the time goes:
time: 216 us; the launch traced here: 211 us
  starting transfers between devices  86.2 us (40%)
  Pallas kernels  46.2 us (21%)
  waiting for transfers between devices  40.7 us (19%)
  other arithmetic  14.2 us (7%)
  local copies, waits for them, and re-layouts  13.4 us (6%)
  matrix products  9.29 us (4%)
    ppermute x27, starting transfers between devices, shift(): return lax.ppermute(value, 'expert', pairs)  46.7 us
    ppermute x27, waiting for transfers between devices, shift(): return lax.ppermute(value, 'expert', pairs)  28 us
    pallas_call x4, Pallas kernels, merge_rows(): pl.pallas_call(merge_kernel, grid=(steps,), in_specs=[pl.BlockSpec((sourc...  19.4 us
    ppermute x6, starting transfers between devices, flip_sum(): return value + lax.ppermute(value, 'expert', pairs)  18.8 us
    pallas_call x2, Pallas kernels, multiply_half(): pl.pallas_call(multiply_kernel, grid=(columns // tile,), in_specs=[pl.Blo...  11.8 us
    unnamed x41, local copies, waits for them, and re-layouts  9.03 us
    ppermute x2, waiting for transfers between devices, from_behind(): lax.ppermute(value, axis, [(source, source + steps) for source in range(l...  6.71 us
    all_to_all x1, starting transfers between devices, conv_rest(): lax.all_to_all(result, 'seq', split_axis=1, concat_axis=0, tiled=True)  6.26 us
  transfers between devices with their start and end apart: 38, of which 13 were waited for; matrix products, arithmetic and copies ran while one was open for 11% of the time, Pallas kernels for 18%

commit v1 on v0

--- a/solution.py
+++ b/solution.py
@@ -9,9 +9,8 @@
 from jax.sharding import PartitionSpec as P
 
 NZ, NY, NC = 8, 4, 2
+REACH = 3
 WIDTHS = (1024, 1024)
-OVERLAP = 2
-PACKED = {1152: 384, 896: 896, 1280: 640, 768: 384, 1024: 512}
 BF = jnp.bfloat16
 F32 = jnp.float32
 VMEM = 40 * 1024 * 1024
@@ -88,42 +87,62 @@
     )(grad_ext, input_ext, kernel)
 
 
-def conv_edges(conv_grad, conv_input, conv_weight):
-    reach = conv_weight.shape[0] - 1
+def conv_edges(conv_grad, conv_input):
     with jax.named_scope("convedges"):
-        input_past = from_behind(conv_input[-reach:], ("expert", "seq"), 1)
-        front = jnp.stack([conv_grad[:reach], conv_input[:reach]], axis=0)
-        front_next = from_behind(front, ("expert", "seq"), -1)
+        past = from_behind(conv_input[-REACH:], ("expert", "seq"), 1)
+        front = jnp.stack([conv_grad[:REACH], conv_input[:REACH]], axis=0)
+        return past, from_behind(front, ("expert", "seq"), -1)
+
+
+def conv_taps(conv_weight):
+    count = lax.axis_size("seq")
     with jax.named_scope("convtaps"):
-        count = lax.axis_size("seq")
         kernel = jnp.broadcast_to(conv_weight[None], (count, *conv_weight.shape))
         kernel = lax.all_to_all(kernel, "seq", split_axis=0, concat_axis=0, tiled=True)
-        kernel = jnp.concatenate([kernel[i] for i in range(count)], axis=1)
-    return input_past, front_next, kernel
-
-
-def conv_local(conv_grad, conv_input, edges):
-    input_past, front_next, kernel = edges
+        return jnp.concatenate([kernel[i] for i in range(count)], axis=1)
+
+
+def conv_local(conv_grad, conv_input, edges, kernel):
+    past, front = edges
     with jax.named_scope("convcore"):
-        return conv_core(conv_grad, conv_input, input_past, front_next[0], front_next[1], kernel)
-
-
-def conv_rest(result, taps):
+        result, taps = conv_core(conv_grad, conv_input, past, front[0], front[1], kernel)
+    return result, taps
+
+
+def taps_move(taps):
     count = lax.axis_size("seq")
-    width = taps.shape[1] // count
+    with jax.named_scope("tapsmove"):
+        width = taps.shape[1] // count
+        taps = jnp.stack([taps[:, i * width : (i + 1) * width] for i in range(count)])
+        taps = lax.all_to_all(taps, "seq", split_axis=0, concat_axis=0, tiled=True)
+        return jnp.sum(taps, axis=0)
+
+
+def keep_kernel(value_ref, out_ref):
+    out_ref[...] = value_ref[...]
+
+
+def conv_move(result):
     with jax.named_scope("convmove"):
         result = lax.all_to_all(result, "seq", split_axis=1, concat_axis=0, tiled=True)
-    with jax.named_scope("tapsmove"):
-        taps = jnp.stack([taps[:, i * width : (i + 1) * width] for i in range(count)])
-        taps = lax.all_to_all(taps, "seq", split_axis=0, concat_axis=0, tiled=True)
-        return result, jnp.sum(taps, axis=0)
+        rows, columns = result.shape
+        block = pl.BlockSpec((rows // 4, columns), lambda i: (i, 0))
+        return pl.pallas_call(
+            keep_kernel,
+            grid=(4,),
+            in_specs=[block],
+            out_specs=block,
+            out_shape=jax.ShapeDtypeStruct(result.shape, BF),
+            cost_estimate=QUICK,
+            name="keep",
+        )(result)
 
 
 PARTNERS = (
     lambda z, y, c: (z, y, c ^ 1),
+    lambda z, y, c: (z ^ 4, y, c),
+    lambda z, y, c: (z ^ 2, y, c),
     lambda z, y, c: (z ^ 1, y, c),
-    lambda z, y, c: (z ^ 2, y, c),
-    lambda z, y, c: (z ^ 4, y, c),
     lambda z, y, c: (z, y ^ 1, c),
     lambda z, y, c: (z, y ^ 2, c),
 )
@@ -232,7 +251,7 @@
         for core in range(NC)
     ]
     for number, place in enumerate(order):
-        columns = turned(info_ref[place], experts)
+        columns = turned(info_ref[(z + place) % NZ], experts)
         first, lane_slot = own_lanes(pair, (z + place) % NZ)
         for source in range(sources):
             picks = (NC * source, NC * source + 1)
@@ -258,28 +277,6 @@
     )(me.reshape(1), info)
 
 
-def multiply_kernel(rows_ref, weight_ref, out_ref):
-    out_ref[...] = jnp.dot(rows_ref[...], weight_ref[0], preferred_element_type=F32).astype(BF)
-
-
-def multiply_half(rows, weight, half, start, columns):
-    size, depth = rows.shape[0] // 2, rows.shape[1]
-    tile = 256 if start % 256 == 0 and columns % 256 == 0 else 128
-    return pl.pallas_call(
-        multiply_kernel,
-        grid=(columns // tile,),
-        in_specs=[
-            pl.BlockSpec((size, depth), lambda i: (half, 0)),
-            pl.BlockSpec((1, depth, tile), lambda i: (0, 0, start // tile + i)),
-        ],
-        out_specs=pl.BlockSpec((size, tile), lambda i: (0, i)),
-        out_shape=jax.ShapeDtypeStruct((size, columns), BF),
-        compiler_params=pltpu.CompilerParams(vmem_limit_bytes=LARGE),
-        cost_estimate=QUICK,
-        name="multiply",
-    )(rows, weight)
-
-
 def pack_kernel(kept_ref, other_ref, *out_refs):
     block = out_refs[0].shape[0] // NC
     for part, ref in enumerate(out_refs):
@@ -287,17 +284,18 @@
         ref[block:] = other_ref[part * block : (part + 1) * block]
 
 
-def pack(kept, other):
-    size, columns = kept.shape
-    tile, pair = PACKED[columns], NC * size // NY
+def pack(kept, other, start, columns):
+    size = kept.shape[0]
+    tile, pair = 512, NC * size // NY
+    cost = pl.CostEstimate(flops=0, bytes_accessed=8 * size * columns, transcendentals=0)
     return pl.pallas_call(
         pack_kernel,
         grid=(columns // tile,),
-        in_specs=[pl.BlockSpec((size, tile), lambda i: (0, i))] * 2,
+        in_specs=[pl.BlockSpec((size, tile), lambda i: (0, start // tile + i))] * 2,
         out_specs=[pl.BlockSpec((pair, tile), lambda i: (0, i))] * NY,
         out_shape=[jax.ShapeDtypeStruct((pair, columns), BF)] * NY,
-        compiler_params=pltpu.CompilerParams(vmem_limit_bytes=VMEM),
-        cost_estimate=QUICK,
+        compiler_params=pltpu.CompilerParams(vmem_limit_bytes=LARGE),
+        cost_estimate=cost,
         name="pack",
     )(kept, other)
 
@@ -311,44 +309,159 @@
     out_ref[...] = total.astype(out_ref.dtype)
 
 
-def merge_rows(matrix, rows, dtype, steps):
+def merge_rows(matrix, rows, dtype):
     sources, places, depth = matrix.shape
     columns = rows[0].shape[1]
-    step = places // steps
+    tile = 256 if columns % 256 == 0 else 128
     return pl.pallas_call(
         merge_kernel,
-        grid=(steps,),
-        in_specs=[pl.BlockSpec((sources, step, depth), lambda i: (0, i, 0))]
-        + [pl.BlockSpec((depth, columns), lambda i: (0, 0))] * sources,
-        out_specs=pl.BlockSpec((step, columns), lambda i: (i, 0)),
+        grid=(columns // tile,),
+        in_specs=[pl.BlockSpec((sources, places, depth), lambda i: (0, 0, 0))]
+        + [pl.BlockSpec((depth, tile), lambda i: (0, i))] * sources,
+        out_specs=pl.BlockSpec((places, tile), lambda i: (0, i)),
         out_shape=jax.ShapeDtypeStruct((places, columns), dtype),
-        compiler_params=pltpu.CompilerParams(vmem_limit_bytes=LARGE if steps > 1 else VMEM),
+        compiler_params=pltpu.CompilerParams(vmem_limit_bytes=VMEM),
         cost_estimate=QUICK,
         name="merge",
     )(matrix, *rows)
 
 
-def z_ring(four, rest, gate):
-    half = four.shape[1] // 2
-    ahead = shift(four[:, :half], dz=1)
-    back = shift(four[:, half:], dz=-1)
-    zeros = jnp.zeros_like(ahead)
-    ahead = jnp.concatenate([ahead, zeros], axis=1)
-    back = jnp.concatenate([zeros, back], axis=1)
-
-    def part(apart):
-        return rest[ORDER.index(apart)]
-
-    for apart in (3, 2, 1):
-        ahead, back = gate(4 - apart, ahead, back)
-        ahead = shift((part(apart) + ahead.astype(F32)).astype(BF), dz=1)
-        back = shift((part(NZ - apart) + back.astype(F32)).astype(BF), dz=-1)
-    return (part(0) + ahead.astype(F32) + back.astype(F32)).astype(BF)
+def ring_kernel(moves, given, *refs):
+    ins, outs = refs[:given], refs[given:]
+    for out, at, pieces in moves:
+        first, start, rows, _ = pieces[0]
+        value = ins[first][start : start + rows].astype(F32)
+        for source, begin, count, offset in pieces[1:]:
+            more = ins[source][begin : begin + count].astype(F32)
+            if count < rows:
+                sides = [value[:offset], value[offset + count :]]
+                sides = [[jnp.zeros_like(side)] if side.shape[0] else [] for side in sides]
+                more = jnp.concatenate([*sides[0], more, *sides[1]], axis=0)
+            value = value + more
+        outs[out][at : at + rows] = value.astype(BF)
+
+
+def ring_step(inputs, moves, out_rows):
+    columns = inputs[0][0].shape[1]
+    tile = columns // 2
+    return pl.pallas_call(
+        functools.partial(ring_kernel, moves, len(inputs)),
+        grid=(2,),
+        in_specs=[
+            pl.BlockSpec((rows, tile), functools.partial(lambda block, i: (block, i), block))
+            for _, rows, block in inputs
+        ],
+        out_specs=[pl.BlockSpec((rows, tile), lambda i: (0, i)) for rows in out_rows],
+        out_shape=[jax.ShapeDtypeStruct((rows, columns), BF) for rows in out_rows],
+        compiler_params=pltpu.CompilerParams(vmem_limit_bytes=VMEM),
+        cost_estimate=QUICK,
+        name="ringstep",
+    )(*[value for value, _, _ in inputs])
+
+
+def last_kernel(done_ref, part_ref, ahead_ref, back_ref, out_ref):
+    early = pl.program_id(0) < pl.num_programs(0) // 2
+
+    @pl.when(early)
+    def _():
+        out_ref[...] = done_ref[...]
+
+    @pl.when(jnp.logical_not(early))
+    def _():
+        total = part_ref[...] + ahead_ref[...].astype(F32) + back_ref[...].astype(F32)
+        out_ref[...] = total.astype(BF)
+
+
+def whole(value):
+    return (value, value.shape[0], 0)
+
+
+def rings(first, second, tokens, hold):
+    half = tokens // 2
+
+    def part(rest, apart):
+        return (rest, tokens, ORDER.index(apart))
+
+    def both(step, ahead, back):
+        ahead, back = hold(step, [ahead, back])
+        with jax.named_scope(f"step{step}"):
+            return shift(ahead, dz=1), shift(back, dz=-1)
+
+    def plain(rest, apart, ahead, back):
+        return ring_step(
+            [part(rest, apart), part(rest, NZ - apart), whole(ahead), whole(back)],
+            [
+                (0, 0, [(0, 0, tokens, 0), (2, 0, tokens, 0)]),
+                (1, 0, [(1, 0, tokens, 0), (3, 0, tokens, 0)]),
+            ],
+            [tokens] * 2,
+        )
+
+    ahead, back = ring_step(
+        [part(first, 4)], [(0, 0, [(0, 0, half, 0)]), (1, 0, [(0, half, half, 0)])], [half] * 2
+    )
+    ahead, back = both(1, ahead, back)
+    ahead, back = ring_step(
+        [part(first, 3), part(first, 5), whole(ahead), whole(back)],
+        [
+            (0, 0, [(0, 0, tokens, 0), (2, 0, half, 0)]),
+            (1, 0, [(1, 0, tokens, 0), (3, 0, half, half)]),
+        ],
+        [tokens] * 2,
+    )
+    ahead, back = both(2, ahead, back)
+    ahead, back = both(3, *plain(first, 2, ahead, back))
+    later = second()
+    ahead, back = ring_step(
+        [part(first, 1), part(first, 7), part(later, 4), whole(ahead), whole(back)],
+        [
+            (0, 0, [(0, 0, tokens, 0), (3, 0, tokens, 0)]),
+            (0, tokens, [(2, 0, half, 0)]),
+            (1, 0, [(1, 0, tokens, 0), (4, 0, tokens, 0)]),
+            (1, tokens, [(2, half, half, 0)]),
+        ],
+        [tokens + half] * 2,
+    )
+    ahead, back = both(4, ahead, back)
+    done, ahead, back = ring_step(
+        [part(first, 0), part(later, 3), part(later, 5), whole(ahead), whole(back)],
+        [
+            (1, 0, [(1, 0, tokens, 0), (3, tokens, half, 0)]),
+            (2, 0, [(2, 0, tokens, 0), (4, tokens, half, half)]),
+            (0, 0, [(0, 0, tokens, 0), (3, 0, tokens, 0), (4, 0, tokens, 0)]),
+        ],
+        [tokens] * 3,
+    )
+    ahead, back = both(5, ahead, back)
+    ahead, back = both(6, *plain(later, 2, ahead, back))
+    ahead, back = both(7, *plain(later, 1, ahead, back))
+    columns = done.shape[1]
+    tile, tiles = columns // 2, 2
+    later_tile = lambda i: jnp.maximum(i - tiles, 0)
+    return pl.pallas_call(
+        last_kernel,
+        grid=(2 * tiles,),
+        in_specs=[
+            pl.BlockSpec((tokens, tile), lambda i: (0, jnp.minimum(i, tiles - 1))),
+            pl.BlockSpec((tokens, tile), lambda i: (ORDER.index(0), later_tile(i))),
+        ]
+        + [pl.BlockSpec((tokens, tile), lambda i: (0, later_tile(i)))] * 2,
+        out_specs=pl.BlockSpec((tokens, tile), lambda i: (0, i)),
+        out_shape=jax.ShapeDtypeStruct((tokens, 2 * columns), BF),
+        compiler_params=pltpu.CompilerParams(vmem_limit_bytes=VMEM),
+        cost_estimate=QUICK,
+        name="last",
+    )(done, later, ahead, back)
 
 
 ROWS_FROM = (0, 1, 3, 2)
-ORDER = (3, 5, 2, 6, 1, 7, 0)
+ORDER = (4, 3, 5, 2, 6, 1, 7, 0)
 BEHIND = (0, -1, 1, -2, 2)
+
+
+def holds(input_grad, taps_at):
+    moved = {step: [taps_at[step - 1]] for step in (4, 5, 6, 7)}
+    return {2: [taps_at[1]], 3: [taps_at[2], input_grad]} | moved
 
 
 def expert_part(
@@ -373,84 +486,67 @@
         rows = sort_rows(rows, y, c)
 
     starts = [sum(WIDTHS[:chunk]) for chunk in range(len(WIDTHS))]
-    def ready(chunk, rows_now):
-        place = (starts[chunk], WIDTHS[chunk])
-        weight = expert_weight[0, :, place[0] : sum(place)]
-        with jax.named_scope(f"multiply{chunk}"):
-            if chunk:
-                out = multiply_half(rows_now, expert_weight, 1, *place)
-                kept = multiply_half(after(rows_now, out), expert_weight, 0, *place)
-            else:
-                out = jnp.dot(rows_now[half:], weight, preferred_element_type=F32).astype(BF)
-                kept = after(rows_now, out)[:half]
-                kept = jnp.dot(kept, weight, preferred_element_type=F32).astype(BF)
-        with jax.named_scope(f"swap{chunk}"):
-            other = shift(out, dc=1)
+
+    with jax.named_scope("multiply"):
+        out = jnp.dot(rows[half:], expert_weight[0], preferred_element_type=F32).astype(BF)
+        kept = after(rows, out)[:half]
+        kept = jnp.dot(kept, expert_weight[0], preferred_element_type=F32).astype(BF)
+    with jax.named_scope("swap"):
+        other = shift(out, dc=1)
+
+    def ready(chunk, *first):
         with jax.named_scope(f"pack{chunk}"):
-            return pack(kept, other), out
-
-    with jax.named_scope("info"):
-        column = jnp.concatenate([routes.T.astype(F32), combine_weights.T], axis=0)[None]
-        column = after(column, rows)
-        column = jnp.concatenate([column, shift(column, dz=-1)], axis=0)
+            return pack(after(kept, *first), other, starts[chunk], WIDTHS[chunk])
 
     def exchange(chunk, parts):
         with jax.named_scope(f"rows{chunk}"):
             return [parts[0]] + [shift(parts[apart], dy=apart) for apart in ROWS_FROM[1:]]
 
     count = len(WIDTHS)
-    parts_first, out = ready(0, rows)
-    parts = [parts_first]
+    edges = conv_edges(after(conv_grad, rows), after(conv_input, rows))
+    parts = [ready(0, *edges)]
+    parts.append(ready(1, *parts[0][1:]))
     arrived = [exchange(0, parts[0])]
     begin = parts[0][1:]
-    edges = conv_edges(
-        after(conv_grad, *begin), after(conv_input, *begin), after(conv_weight, rows)
-    )
     with jax.named_scope("info"):
-        column = after(column, *parts[0][1:])
-        for apart in (2, 4):
-            column = jnp.concatenate([column, shift(column, dz=-apart)], axis=0)
+        own = jnp.concatenate([routes.T.astype(F32), combine_weights.T], axis=0)[None]
+        column = after(jnp.broadcast_to(own, (NZ, *own.shape[1:])), *begin, *parts[1][1:])
+        groups = [
+            [device_at(place, row, core) for place in range(NZ)]
+            for row in range(NY)
+            for core in range(NC)
+        ]
+        column = lax.all_to_all(
+            column, "expert", split_axis=0, concat_axis=0, tiled=True, axis_index_groups=groups
+        )
     with jax.named_scope("gatescolumn"):
-        matrix_four = column_matrix(me, column, (4,), capacity)
-        matrix_rest = column_matrix(me, column, ORDER, capacity)
-    result, taps = conv_local(conv_grad, conv_input, edges)
-    for chunk in range(1, count):
-        parts.append(ready(chunk, after(rows, *parts[-1][1:]))[0])
-        waited = [*arrived[chunk - 1][1:], matrix_rest, result, taps]
-        arrived.append(exchange(chunk, [after(part, *waited) for part in parts[chunk]]))
-    input_grad, taps = conv_rest(after(result, *arrived[0][1:]), after(taps, *arrived[0][1:]))
-
-    results, progress = [], [None] * count
-    for chunk in range(count):
-        slots_now = arrived[chunk]
-        last = chunk + 1 == count
-        if not last:
-            slots_now = [after(value, *parts[chunk + 1][1:]) for value in slots_now]
-        if chunk >= 1:
-            slots_now = [after(value, progress[chunk - 1]) for value in slots_now]
-
-        def gate(step, ahead, back):
-            first = []
-            if step == OVERLAP:
-                progress[chunk] = ahead
-            if not last and step == 2:
-                first += [*arrived[chunk + 1][1:], taps_at[1], input_grad]
-            return [after(value, *first) for value in (ahead, back)] if first else (ahead, back)
-
-        with jax.named_scope(f"merge{chunk}"):
-            four = merge_rows(matrix_four, slots_now, BF, 1)
-            slots_now = [after(value, four) for value in slots_now]
-            rest = merge_rows(matrix_rest, slots_now, F32, 2)
-            rest = rest.reshape(NZ - 1, tokens, WIDTHS[chunk])
-        if chunk == 0:
-            taps_at = [taps]
-            for number, partner in enumerate(PARTNERS):
-                with jax.named_scope(f"taps{number}"):
-                    taps_at.append(flip_sum(taps_at[-1], partner))
-        with jax.named_scope(f"ring{chunk}"):
-            results.append(z_ring(four, rest, gate))
-    weight_grad = taps_at[-1] * (1.0 / math.sqrt(tokens_total))
-    return jnp.concatenate(results, axis=1), input_grad, weight_grad
+        matrix = column_matrix(me, column, ORDER, capacity)
+    kernel = conv_taps(after(conv_weight, *begin))
+    result, taps = conv_local(
+        after(conv_grad, *begin), after(conv_input, *begin), edges, kernel
+    )
+    taps = taps_move(taps) * (1.0 / math.sqrt(tokens_total))
+    waited = [*arrived[0][1:], matrix, taps]
+    arrived.append(exchange(1, [after(part, *waited) for part in parts[1]]))
+    input_grad = conv_move(result)
+
+    taps_at = [taps]
+    for number, partner in enumerate(PARTNERS):
+        with jax.named_scope(f"taps{number}"):
+            taps_at.append(flip_sum(taps_at[-1], partner))
+
+    first = merge_rows(matrix, [after(value, *parts[1][1:]) for value in arrived[0]], F32)
+
+    def second():
+        return merge_rows(matrix, arrived[1], F32)
+
+    before = holds(input_grad, taps_at)
+
+    def hold(step, values):
+        return [after(value, *before[step]) for value in values] if step in before else values
+
+    token_grad = rings(first, second, tokens, hold)
+    return token_grad, input_grad, taps_at[-1]
 
 
 def local(routes, combine_weights, expert_rows, expert_weight, conv_grad, conv_input, conv_weight):

time: 216 us -> 177 us (0.82)
  starting transfers between devices: 86.2 us -> 64.3 us
  other arithmetic: 14.2 us -> 3.28 us
  Pallas kernels: 46.2 us -> 36.5 us
  waiting for transfers between devices: 40.7 us -> 49 us
  local copies, waits for them, and re-layouts: 13.4 us -> 10 us
    ppermute x27 -> x21, starting transfers between devices: 46.7 us -> 27.4 us  [shift(): return lax.ppermute(value, 'expert', pairs)]
    ppermute x6, starting transfers between devices: 18.8 us -> 5.06 us  [flip_sum(): return value + lax.ppermute(value, 'expert', pairs)]
    ppermute x6, waiting for transfers between devices: 3.53 us -> 15.9 us  [flip_sum(): return value + lax.ppermute(value, 'expert', pairs)]
    pallas_call x6 -> x11, Pallas kernels: 31.2 us -> 20.4 us  [the longest x2 13.3 us: merge_rows(): pl.pallas_call(merge_kernel, grid=(columns // tile,), in_specs=[pl.BlockS...]
    all_to_all x3 -> x4, starting transfers between devices: 15.9 us -> 25.7 us  [the longest x1 9.2 us: expert_part(): lax.all_to_all(column, 'expert', split_axis=0, concat_axis=0, tiled=True,...]
    convert_element_type x12 -> x0, other arithmetic: 9.49 us -> none  [the longest x6 5.92 us: z_ring(): ahead = shift((part(apart) + ahead.astype(F32)).astype(BF), dz=1)]
    all_to_all x3 -> x4, waiting for transfers between devices: 2.5 us -> 9.57 us  [the longest x1 7.65 us: expert_part(): lax.all_to_all(column, 'expert', split_axis=0, concat_axis=0, tiled=True,...]
    ppermute x2, waiting for transfers between devices: 6.71 us -> 0.01 us  [from_behind(): lax.ppermute(value, axis, [(source, source + steps) for source in range(l...]
  transfers between devices with their start and end apart: 38 -> 33, of which waited for: 13 -> 17; matrix products, arithmetic and copies ran while one was open for 11% -> 7% of each run, Pallas kernels for 18% -> 16%
where the time goes in v1:
time: 177 us; the launch traced here: 174 us
  starting transfers between devices  64.3 us (36%)
  waiting for transfers between devices  49 us (28%)
  Pallas kernels  36.5 us (21%)
  matrix products  10.2 us (6%)
  local copies, waits for them, and re-layouts  10 us (6%)
  other arithmetic  3.28 us (2%)
    ppermute x21, starting transfers between devices, shift(): return lax.ppermute(value, 'expert', pairs)  27.4 us
    ppermute x21, waiting for transfers between devices, shift(): return lax.ppermute(value, 'expert', pairs)  23.5 us
    ppermute x6, waiting for transfers between devices, flip_sum(): return value + lax.ppermute(value, 'expert', pairs)  15.9 us
    pallas_call x2, Pallas kernels, merge_rows(): pl.pallas_call(merge_kernel, grid=(columns // tile,), in_specs=[pl.BlockS...  13.3 us
    all_to_all x1, starting transfers between devices, expert_part(): lax.all_to_all(column, 'expert', split_axis=0, concat_axis=0, tiled=True,...  9.2 us
    all_to_all x1, waiting for transfers between devices, expert_part(): lax.all_to_all(column, 'expert', split_axis=0, concat_axis=0, tiled=True,...  7.65 us
    pallas_call x2, Pallas kernels, pack(): pl.pallas_call(pack_kernel, grid=(columns // tile,), in_specs=[pl.BlockSp...  7.16 us
    unnamed x28, local copies, waits for them, and re-layouts  6.51 us
  transfers between devices with their start and end apart: 33, of which 17 were waited for; matrix products, arithmetic and copies ran while one was open for 7% of the time, Pallas kernels for 16%

profile of v1, /device:TPU:6, one launch (start us, length us, event | category | flops | bytes accessed | tf_op | source)
XLA Modules:
  0.0 174.4 jit_solution(12313524126987508499)
XLA Ops:
  5.3 4.5 %fusion.4 = bf16[960,2048]{1,0:T(8,128)(2,1)S(1)} fusion(bf16[960,1024]{1,0:T(8,128)(2,1)S(1)} %bitcast.55, bf16[1,1024,2048]{2,1,0:T(8,128)(2,1)S(1)} %copy-done.13), kind=kOutput, calls=%fused_computation.4 | convolution fusion | flops 4028497920 | bytes 10092544 | tf_op jit(solution)/shard_map/multiply/dot_general | solution.py:491
  9.9 4.2 %collective-permute-start = (bf16[3,4096]{1,0:T(4,128)(2,1)S(1)}, bf16[3,4096]{1,0:T(4,128)(2,1)S(1)}, u32[]{:S(2)}, u32[]{:S(2)}) collective-permute-start(bf16[3,4096]{1,0:T(4,128)(2,1)S(1)} %get-tuple-element.112), channel_id=1, source_target_pairs={{0,1},{1,2},{2,3},{3,4},{4,5},{5,6},{6,7},{7,8},{8,9},{9,10},{10,1... | collective-permute-start | bytes 73736 | tf_op jit(solution)/shard_map/convedges/ppermute | solution.py:42
  17.0 5.7 %fusion.7.kept_ref = bf16[960,2048]{1,0:T(8,128)(2,1)} fusion(bf16[1,1024,2048]{2,1,0:T(8,128)(2,1)S(1)} %copy-done.13, bf16[1920,1024]{1,0:T(8,128)(2,1)S(1)} %bitcast.52), kind=kOutput, calls=%fused_computation.5 | convolution fusion | flops 4028497920 | bytes 10092544 | tf_op jit(solution)/shard_map/multiply/dot_general | solution.py:493
  24.7 3.6 %pack.2 = (bf16[480,1024]{1,0:T(8,128)(2,1)}, bf16[480,1024]{1,0:T(8,128)(2,1)}, bf16[480,1024]{1,0:T(8,128)(2,1)}, bf16[480,1024]{1,0:T(8,128)(2,1)}) custom-call(bf16[960,2048]{1,0:T(8,128)(2,1)} %fusion.7.kept_ref, bf16[960,2048]{1,0:T(8,128)(2,1)} %copy-done.8), custom_call_target="tpu_custom_call" | custom-call | bytes 7864320 | tf_op jit(solution)/shard_map/pack0/pack/pallas_call | solution.py:291
  29.6 2.9 %collective-permute-start.5 = (bf16[480,1024]{1,0:T(8,128)(2,1)}, bf16[480,1024]{1,0:T(8,128)(2,1)}, u32[]{:S(2)}, u32[]{:S(2)}) collective-permute-start(bf16[480,1024]{1,0:T(8,128)(2,1)} %get-tuple-element.62), channel_id=1, source_target_pairs={{0,16},{4,20},{8,24},{12,28},{16,0},{20,4},{24,8},{28,12},{32,48},... | collective-permute-start | bytes 2949128 | tf_op jit(solution)/shard_map/rows0/ppermute | solution.py:32
  34.5 5.6 %all-to-all-start.1 = ((f32[4,4,1024]{2,1,0:T(4,128)}), f32[4,4,1024]{2,1,0:T(4,128)S(1)}, u32[]{:S(2)}, u32[]{:S(2)}) async-start(f32[4,4,1024]{2,1,0:T(4,128)} %broadcast_in_dim.5), calls=%async_computation.1 | async-start | bytes 131072 | tf_op jit(solution)/shard_map/convtaps/all_to_all | solution.py:101
  43.6 5.1 %conv.1 = (bf16[128,4096]{1,0:T(8,128)(2,1)S(1)}, f32[4,4096]{1,0:T(4,128)S(1)}) custom-call(bf16[131,4096]{1,0:T(8,128)(2,1)S(1)} %pad_maximum_fusion.grad_ref, bf16[134,4096]{1,0:T(8,128)(2,1)S(1)} %pad_maximum_fusion.1.input_ref, f32[4,4096]{1,0:T(4,128)S(1)} %pad_maximum_fusion.3.taps_ref), custom_call_target="tpu_custom_call" | custom-call | tf_op jit(solution)/shard_map/convcore/conv/pallas_call | solution.py:71
  49.4 5.3 %all-to-all-start.2 = ((f32[4,4,1024]{2,1,0:T(4,128)}), f32[4,4,1024]{2,1,0:T(4,128)S(1)}, u32[]{:S(2)}, u32[]{:S(2)}) async-start(f32[4,4,1024]{2,1,0:T(4,128)} %pad_maximum_fusion.4), calls=%async_computation.2 | async-start | bytes 131072 | tf_op jit(solution)/shard_map/tapsmove/all_to_all | solution.py:117
  54.7 3.6 %pack.3 = (bf16[480,1024]{1,0:T(8,128)(2,1)}, bf16[480,1024]{1,0:T(8,128)(2,1)}, bf16[480,1024]{1,0:T(8,128)(2,1)}, bf16[480,1024]{1,0:T(8,128)(2,1)}) custom-call(bf16[960,2048]{1,0:T(8,128)(2,1)} %fusion.7.kept_ref, bf16[960,2048]{1,0:T(8,128)(2,1)} %copy-done.8), custom_call_target="tpu_custom_call" | custom-call | bytes 7864320 | tf_op jit(solution)/shard_map/pack1/pack/pallas_call | solution.py:291
  59.0 9.2 %all-to-all-start = ((f32[8,20,128]{2,1,0:T(8,128)}), f32[8,20,128]{2,1,0:T(8,128)S(1)}, u32[]{:S(2)}, u32[]{:S(2)}) async-start(f32[8,20,128]{2,1,0:T(8,128)} %broadcast_in_dim.4), calls=%async_computation | async-start | bytes 196608 | tf_op jit(solution)/shard_map/info/all_to_all | solution.py:519
  69.3 7.6 %all-to-all-done.info_ref = f32[8,20,128]{2,1,0:T(8,128)S(1)} async-done(((f32[8,20,128]{2,1,0:T(8,128)}), f32[8,20,128]{2,1,0:T(8,128)S(1)}, u32[]{:S(2)}, u32[]{:S(2)}) %all-to-all-start) | async-done | bytes 81952 | tf_op jit(solution)/shard_map/info/all_to_all | solution.py:519
  76.9 5.6 %all-to-all-start.3 = ((bf16[128,4,1024]{2,0,1:T(8,128)(2,1)}), bf16[128,4,1024]{2,0,1:T(8,128)(2,1)}, u32[]{:S(2)}, u32[]{:S(2)}) async-start(bf16[128,4,1024]{2,0,1:T(8,128)(2,1)} %bitcast.51), calls=%async_computation.3 | async-start | bytes 2097152 | tf_op jit(solution)/shard_map/convmove/all_to_all | solution.py:127
  90.0 6.6 %merge.2.refs_0_.refs_1_ = f32[1024,1024]{1,0:T(8,128)S(1)} custom-call(bf16[4,1024,480]{2,1,0:T(8,128)(2,1)S(1)} %gatescolumn.1.matrix_ref, bf16[480,1024]{1,0:T(8,128)(2,1)S(1)} %copy-done.7, bf16[480,1024]{1,0:T(8,128)(2,1)} %collective-permute-done.3.refs_1_, bf16[480,1024]{1,0:T(8,128)(2,1)} %collective-permute-done.4.refs_2_, ...), custom_call_target="tpu_custom_call" | custom-call | tf_op jit(solution)/shard_map/merge/pallas_call | solution.py:316
  97.4 2.7 %collective-permute-start.10 = (bf16[64,1024]{1,0:T(8,128)(2,1)S(1)}, bf16[64,1024]{1,0:T(8,128)(2,1)S(1)}, u32[]{:S(2)}, u32[]{:S(2)}) collective-permute-start(bf16[64,1024]{1,0:T(8,128)(2,1)S(1)} %get-tuple-element.84), channel_id=1, source_target_pairs={{0,224},{4,228},{8,232},{12,236},{16,240},{20,244},{24,248},{28,25... | collective-permute-start | bytes 393224 | tf_op jit(solution)/shard_map/step1/ppermute | solution.py:32
  100.1 3.9 %collective-permute-done.9.refs_2_ = bf16[64,1024]{1,0:T(8,128)(2,1)S(1)} collective-permute-done((bf16[64,1024]{1,0:T(8,128)(2,1)S(1)}, bf16[64,1024]{1,0:T(8,128)(2,1)S(1)}, u32[]{:S(2)}, u32[]{:S(2)}) %collective-permute-start.9) | collective-permute-done | bytes 131104 | tf_op jit(solution)/shard_map/step1/ppermute | solution.py:32
  104.7 2.6 %collective-permute-start.13 = (bf16[128,1024]{1,0:T(8,128)(2,1)S(1)}, bf16[128,1024]{1,0:T(8,128)(2,1)S(1)}, u32[]{:S(2)}, u32[]{:S(2)}) collective-permute-start(bf16[128,1024]{1,0:T(8,128)(2,1)S(1)} %get-tuple-element.88), channel_id=1, source_target_pairs={{0,224},{4,228},{8,232},{12,236},{16,240},{20,244},{24,248},{28,25... | collective-permute-start | bytes 786440 | tf_op jit(solution)/shard_map/step2/ppermute | solution.py:32
  107.3 4.4 %collective-permute-done.14 = f32[4,1024]{1,0:T(4,128)S(1)} collective-permute-done((f32[4,1024]{1,0:T(4,128)S(1)}, f32[4,1024]{1,0:T(4,128)S(1)}, u32[]{:S(2)}, u32[]{:S(2)}) %collective-permute-start.14) | collective-permute-done | bytes 16416 | tf_op jit(solution)/shard_map/taps1/ppermute | solution.py:158
  114.1 3.4 %keep.1 = bf16[512,1024]{1,0:T(8,128)(2,1)} custom-call(bf16[512,1024]{1,0:T(8,128)(2,1)} %bitcast.22.value_ref), custom_call_target="tpu_custom_call" | custom-call | tf_op jit(solution)/shard_map/convmove/keep/pallas_call | solution.py:130
  125.7 6.7 %merge.3.refs_2_.refs_1_.refs_0_.part_ref = f32[1024,1024]{1,0:T(8,128)S(1)} custom-call(bf16[4,1024,480]{2,1,0:T(8,128)(2,1)S(1)} %copy-done.4, bf16[480,1024]{1,0:T(8,128)(2,1)S(1)} %copy-done.6, bf16[480,1024]{1,0:T(8,128)(2,1)S(1)} %collective-permute-done.6.refs_1_, bf16[480,1024]{1,0:T(8,128)(2,1)S(1)} %collective-permute-done.7.refs_2_, ...), custom_call_target="tpu_custom_call" | custom-call | tf_op jit(solution)/shard_map/merge/pallas_call | solution.py:316
  135.5 5.4 %collective-permute-done.20 = f32[4,1024]{1,0:T(4,128)S(1)} collective-permute-done((f32[4,1024]{1,0:T(4,128)S(1)}, f32[4,1024]{1,0:T(4,128)S(1)}, u32[]{:S(2)}, u32[]{:S(2)}) %collective-permute-start.20) | collective-permute-done | bytes 16416 | tf_op jit(solution)/shard_map/taps3/ppermute | solution.py:158
  140.9 3.2 %collective-permute-done.18.refs_3_ = bf16[192,1024]{1,0:T(8,128)(2,1)S(1)} collective-permute-done((bf16[192,1024]{1,0:T(8,128)(2,1)S(1)}, bf16[192,1024]{1,0:T(8,128)(2,1)S(1)}, u32[]{:S(2)}, u32[]{:S(2)}) %collective-permute-start.18) | collective-permute-done | bytes 393248 | tf_op jit(solution)/shard_map/step4/ppermute | solution.py:32
  151.2 3.1 %collective-permute-done.21.refs_2_ = bf16[128,1024]{1,0:T(8,128)(2,1)S(1)} collective-permute-done((bf16[128,1024]{1,0:T(8,128)(2,1)S(1)}, bf16[128,1024]{1,0:T(8,128)(2,1)S(1)}, u32[]{:S(2)}, u32[]{:S(2)}) %collective-permute-start.21) | collective-permute-done | bytes 262176 | tf_op jit(solution)/shard_map/step5/ppermute | solution.py:32
  158.4 3.5 %collective-permute-done.26 = f32[4,1024]{1,0:T(4,128)S(1)} collective-permute-done((f32[4,1024]{1,0:T(4,128)S(1)}, f32[4,1024]{1,0:T(4,128)S(1)}, u32[]{:S(2)}, u32[]{:S(2)}) %collective-permute-start.26) | collective-permute-done | bytes 16416 | tf_op jit(solution)/shard_map/taps5/ppermute | solution.py:158
  166.9 4.3 %collective-permute-done.28.back_ref = bf16[128,1024]{1,0:T(8,128)(2,1)S(1)} collective-permute-done((bf16[128,1024]{1,0:T(8,128)(2,1)S(1)}, bf16[128,1024]{1,0:T(8,128)(2,1)S(1)}, u32[]{:S(2)}, u32[]{:S(2)}) %collective-permute-start.28) | collective-permute-done | bytes 262176 | tf_op jit(solution)/shard_map/step7/ppermute | solution.py:32
  (116 shorter events, 60.7 us)
Async XLA Ops:
  9.8 13.0 %collective-permute-start.2 = (bf16[960,2048]{1,0:T(8,128)(2,1)S(1)}, bf16[960,2048]{1,0:T(8,128)(2,1)S(1)}, u32[]{:S(2)}, u32[]{:S(2)}) collective-permute-start(bf16[960,2048]{1,0:T(8,128)(2,1)S(1)} %fusion.4), channel_id=1, source_target_pairs={{0,4},{4,0},{8,12},{12,8},{16,20},{20,16},{24,28},{28,24},{32,36},... | collective-permute-start | bytes 11796488 | tf_op jit(solution)/shard_map/swap/ppermute | solution.py:32
  9.9 12.8 %collective-permute-start = (bf16[3,4096]{1,0:T(4,128)(2,1)S(1)}, bf16[3,4096]{1,0:T(4,128)(2,1)S(1)}, u32[]{:S(2)}, u32[]{:S(2)}) collective-permute-start(bf16[3,4096]{1,0:T(4,128)(2,1)S(1)} %get-tuple-element.112), channel_id=1, source_target_pairs={{0,1},{1,2},{2,3},{3,4},{4,5},{5,6},{6,7},{7,8},{8,9},{9,10},{10,1... | collective-permute-start | bytes 73736 | tf_op jit(solution)/shard_map/convedges/ppermute | solution.py:42
  15.1 7.7 %collective-permute-start.1 = (bf16[2,3,4096]{2,1,0:T(4,128)(2,1)S(1)}, bf16[2,3,4096]{2,1,0:T(4,128)(2,1)S(1)}, u32[]{:S(2)}, u32[]{:S(2)}) collective-permute-start(bf16[2,3,4096]{2,1,0:T(4,128)(2,1)S(1)} %pad_maximum_fusion.2), channel_id=1, source_target_pairs={{1,0},{2,1},{3,2},{4,3},{5,4},{6,5},{7,6},{8,7},{9,8},{10,9},{11,1... | collective-permute-start | bytes 147464 | tf_op jit(solution)/shard_map/convedges/ppermute | solution.py:42
  28.3 56.4 %collective-permute-start.3 = (bf16[480,1024]{1,0:T(8,128)(2,1)}, bf16[480,1024]{1,0:T(8,128)(2,1)}, u32[]{:S(2)}, u32[]{:S(2)}) collective-permute-start(bf16[480,1024]{1,0:T(8,128)(2,1)} %get-tuple-element.61), channel_id=1, source_target_pairs={{0,8},{4,12},{8,16},{12,20},{16,24},{20,28},{24,0},{28,4},{32,40},... | collective-permute-start | bytes 2949128 | tf_op jit(solution)/shard_map/rows0/ppermute | solution.py:32
  29.6 55.2 %collective-permute-start.5 = (bf16[480,1024]{1,0:T(8,128)(2,1)}, bf16[480,1024]{1,0:T(8,128)(2,1)}, u32[]{:S(2)}, u32[]{:S(2)}) collective-permute-start(bf16[480,1024]{1,0:T(8,128)(2,1)} %get-tuple-element.62), channel_id=1, source_target_pairs={{0,16},{4,20},{8,24},{12,28},{16,0},{20,4},{24,8},{28,12},{32,48},... | collective-permute-start | bytes 2949128 | tf_op jit(solution)/shard_map/rows0/ppermute | solution.py:32
  32.5 52.3 %collective-permute-start.4 = (bf16[480,1024]{1,0:T(8,128)(2,1)}, bf16[480,1024]{1,0:T(8,128)(2,1)}, u32[]{:S(2)}, u32[]{:S(2)}) collective-permute-start(bf16[480,1024]{1,0:T(8,128)(2,1)} %get-tuple-element.63), channel_id=1, source_target_pairs={{0,24},{4,28},{8,0},{12,4},{16,8},{20,12},{24,16},{28,20},{32,56},... | collective-permute-start | bytes 2949128 | tf_op jit(solution)/shard_map/rows0/ppermute | solution.py:32
  34.5 9.1 %all-to-all-start.1 = ((f32[4,4,1024]{2,1,0:T(4,128)}), f32[4,4,1024]{2,1,0:T(4,128)S(1)}, u32[]{:S(2)}, u32[]{:S(2)}) async-start(f32[4,4,1024]{2,1,0:T(4,128)} %broadcast_in_dim.5), calls=%async_computation.1 | async-start | bytes 131072 | tf_op jit(solution)/shard_map/convtaps/all_to_all | solution.py:101
  49.4 9.6 %all-to-all-start.2 = ((f32[4,4,1024]{2,1,0:T(4,128)}), f32[4,4,1024]{2,1,0:T(4,128)S(1)}, u32[]{:S(2)}, u32[]{:S(2)}) async-start(f32[4,4,1024]{2,1,0:T(4,128)} %pad_maximum_fusion.4), calls=%async_computation.2 | async-start | bytes 131072 | tf_op jit(solution)/shard_map/tapsmove/all_to_all | solution.py:117
  59.0 17.9 %all-to-all-start = ((f32[8,20,128]{2,1,0:T(8,128)}), f32[8,20,128]{2,1,0:T(8,128)S(1)}, u32[]{:S(2)}, u32[]{:S(2)}) async-start(f32[8,20,128]{2,1,0:T(8,128)} %broadcast_in_dim.4), calls=%async_computation | async-start | bytes 196608 | tf_op jit(solution)/shard_map/info/all_to_all | solution.py:519
  76.9 37.2 %all-to-all-start.3 = ((bf16[128,4,1024]{2,0,1:T(8,128)(2,1)}), bf16[128,4,1024]{2,0,1:T(8,128)(2,1)}, u32[]{:S(2)}, u32[]{:S(2)}) async-start(bf16[128,4,1024]{2,0,1:T(8,128)(2,1)} %bitcast.51), calls=%async_computation.3 | async-start | bytes 2097152 | tf_op jit(solution)/shard_map/convmove/all_to_all | solution.py:127
  84.8 41.0 %collective-permute-start.6 = (bf16[480,1024]{1,0:T(8,128)(2,1)}, bf16[480,1024]{1,0:T(8,128)(2,1)S(1)}, u32[]{:S(2)}, u32[]{:S(2)}) collective-permute-start(bf16[480,1024]{1,0:T(8,128)(2,1)} %get-tuple-element.80), channel_id=1, source_target_pairs={{0,8},{4,12},{8,16},{12,20},{16,24},{20,28},{24,0},{28,4},{32,40},... | collective-permute-start | bytes 2949128 | tf_op jit(solution)/shard_map/rows1/ppermute | solution.py:32
  85.9 39.8 %collective-permute-start.7 = (bf16[480,1024]{1,0:T(8,128)(2,1)}, bf16[480,1024]{1,0:T(8,128)(2,1)S(1)}, u32[]{:S(2)}, u32[]{:S(2)}) collective-permute-start(bf16[480,1024]{1,0:T(8,128)(2,1)} %get-tuple-element.81), channel_id=1, source_target_pairs={{0,24},{4,28},{8,0},{12,4},{16,8},{20,12},{24,16},{28,20},{32,56},... | collective-permute-start | bytes 2949128 | tf_op jit(solution)/shard_map/rows1/ppermute | solution.py:32
  88.2 37.5 %collective-permute-start.8 = (bf16[480,1024]{1,0:T(8,128)(2,1)}, bf16[480,1024]{1,0:T(8,128)(2,1)}, u32[]{:S(2)}, u32[]{:S(2)}) collective-permute-start(bf16[480,1024]{1,0:T(8,128)(2,1)} %get-tuple-element.82), channel_id=1, source_target_pairs={{0,16},{4,20},{8,24},{12,28},{16,0},{20,4},{24,8},{28,12},{32,48},... | collective-permute-start | bytes 2949128 | tf_op jit(solution)/shard_map/rows1/ppermute | solution.py:32
  104.0 7.8 %collective-permute-start.14 = (f32[4,1024]{1,0:T(4,128)S(1)}, f32[4,1024]{1,0:T(4,128)S(1)}, u32[]{:S(2)}, u32[]{:S(2)}) collective-permute-start(f32[4,1024]{1,0:T(4,128)S(1)} %fusion.31), channel_id=1, source_target_pairs={{0,128},{4,132},{8,136},{12,140},{16,144},{20,148},{24,152},{28,15... | collective-permute-start | bytes 49160 | tf_op jit(solution)/shard_map/taps1/ppermute | solution.py:158
  104.7 8.1 %collective-permute-start.13 = (bf16[128,1024]{1,0:T(8,128)(2,1)S(1)}, bf16[128,1024]{1,0:T(8,128)(2,1)S(1)}, u32[]{:S(2)}, u32[]{:S(2)}) collective-permute-start(bf16[128,1024]{1,0:T(8,128)(2,1)S(1)} %get-tuple-element.88), channel_id=1, source_target_pairs={{0,224},{4,228},{8,232},{12,236},{16,240},{20,244},{24,248},{28,25... | collective-permute-start | bytes 786440 | tf_op jit(solution)/shard_map/step2/ppermute | solution.py:32
  111.7 7.9 %collective-permute-start.12 = (bf16[128,1024]{1,0:T(8,128)(2,1)S(1)}, bf16[128,1024]{1,0:T(8,128)(2,1)S(1)}, u32[]{:S(2)}, u32[]{:S(2)}) collective-permute-start(bf16[128,1024]{1,0:T(8,128)(2,1)S(1)} %get-tuple-element.86), channel_id=1, source_target_pairs={{0,32},{4,36},{8,40},{12,44},{16,48},{20,52},{24,56},{28,60},{32,6... | collective-permute-start | bytes 786440 | tf_op jit(solution)/shard_map/step2/ppermute | solution.py:32
  112.8 9.7 %collective-permute-start.17 = (f32[4,1024]{1,0:T(4,128)S(1)}, f32[4,1024]{1,0:T(4,128)S(1)}, u32[]{:S(2)}, u32[]{:S(2)}) collective-permute-start(f32[4,1024]{1,0:T(4,128)S(1)} %add.89), channel_id=1, source_target_pairs={{0,64},{4,68},{8,72},{12,76},{16,80},{20,84},{24,88},{28,92},{32,9... | collective-permute-start | bytes 49160 | tf_op jit(solution)/shard_map/taps2/ppermute | solution.py:158
  122.1 10.4 %collective-permute-start.16 = (bf16[128,1024]{1,0:T(8,128)(2,1)S(1)}, bf16[128,1024]{1,0:T(8,128)(2,1)S(1)}, u32[]{:S(2)}, u32[]{:S(2)}) collective-permute-start(bf16[128,1024]{1,0:T(8,128)(2,1)S(1)} %get-tuple-element.93), channel_id=1, source_target_pairs={{0,224},{4,228},{8,232},{12,236},{16,240},{20,244},{24,248},{28,25... | collective-permute-start | bytes 786440 | tf_op jit(solution)/shard_map/step3/ppermute | solution.py:32
  122.5 10.0 %collective-permute-start.15 = (bf16[128,1024]{1,0:T(8,128)(2,1)S(1)}, bf16[128,1024]{1,0:T(8,128)(2,1)S(1)}, u32[]{:S(2)}, u32[]{:S(2)}) collective-permute-start(bf16[128,1024]{1,0:T(8,128)(2,1)S(1)} %get-tuple-element.91), channel_id=1, source_target_pairs={{0,32},{4,36},{8,40},{12,44},{16,48},{20,52},{24,56},{28,60},{32,6... | collective-permute-start | bytes 786440 | tf_op jit(solution)/shard_map/step3/ppermute | solution.py:32
  132.9 8.0 %collective-permute-start.19 = (bf16[192,1024]{1,0:T(8,128)(2,1)S(1)}, bf16[192,1024]{1,0:T(8,128)(2,1)S(1)}, u32[]{:S(2)}, u32[]{:S(2)}) collective-permute-start(bf16[192,1024]{1,0:T(8,128)(2,1)S(1)} %get-tuple-element.97), channel_id=1, source_target_pairs={{0,224},{4,228},{8,232},{12,236},{16,240},{20,244},{24,248},{28,25... | collective-permute-start | bytes 1179656 | tf_op jit(solution)/shard_map/step4/ppermute | solution.py:32
  135.1 9.0 %collective-permute-start.18 = (bf16[192,1024]{1,0:T(8,128)(2,1)S(1)}, bf16[192,1024]{1,0:T(8,128)(2,1)S(1)}, u32[]{:S(2)}, u32[]{:S(2)}) collective-permute-start(bf16[192,1024]{1,0:T(8,128)(2,1)S(1)} %get-tuple-element.95), channel_id=1, source_target_pairs={{0,32},{4,36},{8,40},{12,44},{16,48},{20,52},{24,56},{28,60},{32,6... | collective-permute-start | bytes 1179656 | tf_op jit(solution)/shard_map/step4/ppermute | solution.py:32
  145.7 8.6 %collective-permute-start.21 = (bf16[128,1024]{1,0:T(8,128)(2,1)S(1)}, bf16[128,1024]{1,0:T(8,128)(2,1)S(1)}, u32[]{:S(2)}, u32[]{:S(2)}) collective-permute-start(bf16[128,1024]{1,0:T(8,128)(2,1)S(1)} %get-tuple-element.100), channel_id=1, source_target_pairs={{0,32},{4,36},{8,40},{12,44},{16,48},{20,52},{24,56},{28,60},{32,6... | collective-permute-start | bytes 786440 | tf_op jit(solution)/shard_map/step5/ppermute | solution.py:32
  154.6 8.6 %collective-permute-start.25 = (bf16[128,1024]{1,0:T(8,128)(2,1)S(1)}, bf16[128,1024]{1,0:T(8,128)(2,1)S(1)}, u32[]{:S(2)}, u32[]{:S(2)}) collective-permute-start(bf16[128,1024]{1,0:T(8,128)(2,1)S(1)} %get-tuple-element.106), channel_id=1, source_target_pairs={{0,224},{4,228},{8,232},{12,236},{16,240},{20,244},{24,248},{28,25... | collective-permute-start | bytes 786440 | tf_op jit(solution)/shard_map/step6/ppermute | solution.py:32
  154.7 9.8 %collective-permute-start.24 = (bf16[128,1024]{1,0:T(8,128)(2,1)S(1)}, bf16[128,1024]{1,0:T(8,128)(2,1)S(1)}, u32[]{:S(2)}, u32[]{:S(2)}) collective-permute-start(bf16[128,1024]{1,0:T(8,128)(2,1)S(1)} %get-tuple-element.104), channel_id=1, source_target_pairs={{0,32},{4,36},{8,40},{12,44},{16,48},{20,52},{24,56},{28,60},{32,6... | collective-permute-start | bytes 786440 | tf_op jit(solution)/shard_map/step6/ppermute | solution.py:32
  (23 other events, 144.2 us)

commit v2 on v1

--- a/solution.py
+++ b/solution.py
@@ -15,6 +15,7 @@
 F32 = jnp.float32
 VMEM = 40 * 1024 * 1024
 LARGE = 58 * 1024 * 1024
+FILLS = pl.CostEstimate(flops=0, bytes_accessed=12_000_000, transcendentals=0)
 QUICK = pl.CostEstimate(flops=0, bytes_accessed=0, transcendentals=0)
 
 
@@ -82,7 +83,7 @@
             jax.ShapeDtypeStruct((taps, channels), F32),
         ],
         compiler_params=pltpu.CompilerParams(vmem_limit_bytes=VMEM),
-        cost_estimate=QUICK,
+        cost_estimate=FILLS,
         name="conv",
     )(grad_ext, input_ext, kernel)
 
@@ -272,7 +273,7 @@
         ),
         out_shape=jax.ShapeDtypeStruct((sources, len(order) * tokens, pair), BF),
         compiler_params=pltpu.CompilerParams(vmem_limit_bytes=VMEM),
-        cost_estimate=QUICK,
+        cost_estimate=FILLS,
         name="gatescolumn",
     )(me.reshape(1), info)
 
@@ -510,7 +511,7 @@
     begin = parts[0][1:]
     with jax.named_scope("info"):
         own = jnp.concatenate([routes.T.astype(F32), combine_weights.T], axis=0)[None]
-        column = after(jnp.broadcast_to(own, (NZ, *own.shape[1:])), *begin, *parts[1][1:])
+        column = after(jnp.broadcast_to(own, (NZ, *own.shape[1:])), *begin)
         groups = [
             [device_at(place, row, core) for place in range(NZ)]
             for row in range(NY)
@@ -525,10 +526,10 @@
     result, taps = conv_local(
         after(conv_grad, *begin), after(conv_input, *begin), edges, kernel
     )
-    taps = taps_move(taps) * (1.0 / math.sqrt(tokens_total))
+    taps = taps_move(after(taps, column)) * (1.0 / math.sqrt(tokens_total))
+    input_grad = conv_move(result)
     waited = [*arrived[0][1:], matrix, taps]
     arrived.append(exchange(1, [after(part, *waited) for part in parts[1]]))
-    input_grad = conv_move(result)
 
     taps_at = [taps]
     for number, partner in enumerate(PARTNERS):

time: 177 us -> 175 us (0.989); the launches traced: 174 us -> 175 us
  local copies, waits for them, and re-layouts: 10 us -> 14.2 us
  waiting for transfers between devices: 49 us -> 46.3 us
    unnamed x28 -> x30, local copies, waits for them, and re-layouts: 6.51 us -> 10.7 us
    all_to_all x1, waiting for transfers between devices: 7.65 us -> 3.59 us  [expert_part(): lax.all_to_all(column, 'expert', split_axis=0, concat_axis=0, tiled=True,...]
    ppermute x6, waiting for transfers between devices: 15.9 us -> 19.5 us  [flip_sum(): return value + lax.ppermute(value, 'expert', pairs)]
  transfers between devices with their start and end apart: 33 -> 33, of which waited for: 17 -> 15; matrix products, arithmetic and copies ran while one was open for 7% -> 7% of each run, Pallas kernels for 16% -> 16%
where the time goes in v2:
time: 175 us
  starting transfers between devices  63 us (36%)
  waiting for transfers between devices  46.3 us (26%)
  Pallas kernels  36.5 us (21%)
  local copies, waits for them, and re-layouts  14.2 us (8%)
  matrix products  10.2 us (6%)
  other arithmetic  3.28 us (2%)
    ppermute x21, starting transfers between devices, shift(): return lax.ppermute(value, 'expert', pairs)  27.7 us
    ppermute x21, waiting for transfers between devices, shift(): return lax.ppermute(value, 'expert', pairs)  22 us
    ppermute x6, waiting for transfers between devices, flip_sum(): return value + lax.ppermute(value, 'expert', pairs)  19.5 us
    pallas_call x2, Pallas kernels, merge_rows(): pl.pallas_call(merge_kernel, grid=(columns // tile,), in_specs=[pl.BlockS...  13.3 us
    unnamed x30, local copies, waits for them, and re-layouts  10.7 us
    all_to_all x1, starting transfers between devices, expert_part(): lax.all_to_all(column, 'expert', split_axis=0, concat_axis=0, tiled=True,...  9.2 us
    pallas_call x2, Pallas kernels, pack(): pl.pallas_call(pack_kernel, grid=(columns // tile,), in_specs=[pl.BlockSp...  7.17 us
    ppermute x2, starting transfers between devices, from_behind(): lax.ppermute(value, axis, [(source, source + steps) for source in range(l...  6.13 us
  transfers between devices with their start and end apart: 33, of which 15 were waited for; matrix products, arithmetic and copies ran while one was open for 7% of the time, Pallas kernels for 16%

profile of v2, /device:TPU:6, one launch (start us, length us, event | category | flops | bytes accessed | tf_op | source)
XLA Modules:
  0.0 174.6 jit_solution(17972201734815536287)
XLA Ops:
  5.3 4.5 %fusion.4 = bf16[960,2048]{1,0:T(8,128)(2,1)S(1)} fusion(bf16[960,1024]{1,0:T(8,128)(2,1)S(1)} %bitcast.55, bf16[1,1024,2048]{2,1,0:T(8,128)(2,1)S(1)} %copy-done.14), kind=kOutput, calls=%fused_computation.4 | convolution fusion | flops 4028497920 | bytes 10092544 | tf_op jit(solution)/shard_map/multiply/dot_general | solution.py:492
  9.9 4.2 %collective-permute-start = (bf16[3,4096]{1,0:T(4,128)(2,1)S(1)}, bf16[3,4096]{1,0:T(4,128)(2,1)S(1)}, u32[]{:S(2)}, u32[]{:S(2)}) collective-permute-start(bf16[3,4096]{1,0:T(4,128)(2,1)S(1)} %get-tuple-element.114), channel_id=1, source_target_pairs={{0,1},{1,2},{2,3},{3,4},{4,5},{5,6},{6,7},{7,8},{8,9},{9,10},{10,1... | collective-permute-start | bytes 73736 | tf_op jit(solution)/shard_map/convedges/ppermute | solution.py:43
  17.0 5.7 %fusion.7.kept_ref = bf16[960,2048]{1,0:T(8,128)(2,1)} fusion(bf16[1,1024,2048]{2,1,0:T(8,128)(2,1)S(1)} %copy-done.14, bf16[1920,1024]{1,0:T(8,128)(2,1)S(1)} %bitcast.52), kind=kOutput, calls=%fused_computation.5 | convolution fusion | flops 4028497920 | bytes 10092544 | tf_op jit(solution)/shard_map/multiply/dot_general | solution.py:494
  24.8 3.6 %pack.2 = (bf16[480,1024]{1,0:T(8,128)(2,1)}, bf16[480,1024]{1,0:T(8,128)(2,1)}, bf16[480,1024]{1,0:T(8,128)(2,1)}, bf16[480,1024]{1,0:T(8,128)(2,1)}) custom-call(bf16[960,2048]{1,0:T(8,128)(2,1)} %fusion.7.kept_ref, bf16[960,2048]{1,0:T(8,128)(2,1)} %copy-done.9), custom_call_target="tpu_custom_call" | custom-call | bytes 7864320 | tf_op jit(solution)/shard_map/pack0/pack/pallas_call | solution.py:292
  29.6 2.9 %collective-permute-start.5 = (bf16[480,1024]{1,0:T(8,128)(2,1)}, bf16[480,1024]{1,0:T(8,128)(2,1)}, u32[]{:S(2)}, u32[]{:S(2)}) collective-permute-start(bf16[480,1024]{1,0:T(8,128)(2,1)} %get-tuple-element.63), channel_id=1, source_target_pairs={{0,16},{4,20},{8,24},{12,28},{16,0},{20,4},{24,8},{28,12},{32,48},... | collective-permute-start | bytes 2949128 | tf_op jit(solution)/shard_map/rows0/ppermute | solution.py:33
  34.5 5.6 %all-to-all-start.1 = ((f32[4,4,1024]{2,1,0:T(4,128)}), f32[4,4,1024]{2,1,0:T(4,128)S(1)}, u32[]{:S(2)}, u32[]{:S(2)}) async-start(f32[4,4,1024]{2,1,0:T(4,128)} %broadcast_in_dim.5), calls=%async_computation.1 | async-start | bytes 131072 | tf_op jit(solution)/shard_map/convtaps/all_to_all | solution.py:102
  43.6 9.2 %all-to-all-start = ((f32[8,20,128]{2,1,0:T(8,128)}), f32[8,20,128]{2,1,0:T(8,128)S(1)}, u32[]{:S(2)}, u32[]{:S(2)}) async-start(f32[8,20,128]{2,1,0:T(8,128)} %broadcast_in_dim.4), calls=%async_computation | async-start | bytes 196608 | tf_op jit(solution)/shard_map/info/all_to_all | solution.py:520
  52.9 5.1 %conv.1 = (bf16[128,4096]{1,0:T(8,128)(2,1)S(1)}, f32[4,4096]{1,0:T(4,128)S(1)}) custom-call(bf16[131,4096]{1,0:T(8,128)(2,1)S(1)} %pad_maximum_fusion.grad_ref, bf16[134,4096]{1,0:T(8,128)(2,1)S(1)} %pad_maximum_fusion.1.input_ref, f32[4,4096]{1,0:T(4,128)S(1)} %pad_maximum_fusion.3.taps_ref), custom_call_target="tpu_custom_call" | custom-call | bytes 12000000 | tf_op jit(solution)/shard_map/convcore/conv/pallas_call | solution.py:72
  58.0 3.6 %all-to-all-done.info_ref = f32[8,20,128]{2,1,0:T(8,128)S(1)} async-done(((f32[8,20,128]{2,1,0:T(8,128)}), f32[8,20,128]{2,1,0:T(8,128)S(1)}, u32[]{:S(2)}, u32[]{:S(2)}) %all-to-all-start) | async-done | bytes 81952 | tf_op jit(solution)/shard_map/info/all_to_all | solution.py:520
  62.2 5.3 %all-to-all-start.2 = ((f32[4,4,1024]{2,1,0:T(4,128)}), f32[4,4,1024]{2,1,0:T(4,128)S(1)}, u32[]{:S(2)}, u32[]{:S(2)}) async-start(f32[4,4,1024]{2,1,0:T(4,128)} %pad_maximum_fusion.4), calls=%async_computation.2 | async-start | bytes 131072 | tf_op jit(solution)/shard_map/tapsmove/all_to_all | solution.py:118
  67.5 3.6 %pack.3 = (bf16[480,1024]{1,0:T(8,128)(2,1)}, bf16[480,1024]{1,0:T(8,128)(2,1)}, bf16[480,1024]{1,0:T(8,128)(2,1)}, bf16[480,1024]{1,0:T(8,128)(2,1)}) custom-call(bf16[960,2048]{1,0:T(8,128)(2,1)} %fusion.7.kept_ref, bf16[960,2048]{1,0:T(8,128)(2,1)} %copy-done.9), custom_call_target="tpu_custom_call" | custom-call | bytes 7864320 | tf_op jit(solution)/shard_map/pack1/pack/pallas_call | solution.py:292
  76.4 4.8 %all-to-all-start.3 = ((bf16[128,4,1024]{2,0,1:T(8,128)(2,1)}), bf16[128,4,1024]{2,0,1:T(8,128)(2,1)}, u32[]{:S(2)}, u32[]{:S(2)}) async-start(bf16[128,4,1024]{2,0,1:T(8,128)(2,1)} %bitcast.51), calls=%async_computation.3 | async-start | bytes 2097152 | tf_op jit(solution)/shard_map/convmove/all_to_all | solution.py:128
  88.6 6.6 %merge.2.refs_0_.refs_1_ = f32[1024,1024]{1,0:T(8,128)S(1)} custom-call(bf16[4,1024,480]{2,1,0:T(8,128)(2,1)S(1)} %copy-done.4, bf16[480,1024]{1,0:T(8,128)(2,1)S(1)} %copy-done.8, bf16[480,1024]{1,0:T(8,128)(2,1)} %collective-permute-done.3.refs_1_, bf16[480,1024]{1,0:T(8,128)(2,1)} %collective-permute-done.4.refs_2_, ...), custom_call_target="tpu_custom_call" | custom-call | tf_op jit(solution)/shard_map/merge/pallas_call | solution.py:317
  98.8 3.9 %collective-permute-done.9.refs_2_ = bf16[64,1024]{1,0:T(8,128)(2,1)S(1)} collective-permute-done((bf16[64,1024]{1,0:T(8,128)(2,1)S(1)}, bf16[64,1024]{1,0:T(8,128)(2,1)S(1)}, u32[]{:S(2)}, u32[]{:S(2)}) %collective-permute-start.9) | collective-permute-done | bytes 131104 | tf_op jit(solution)/shard_map/step1/ppermute | solution.py:33
  105.9 4.3 %collective-permute-done.14 = f32[4,1024]{1,0:T(4,128)S(1)} collective-permute-done((f32[4,1024]{1,0:T(4,128)S(1)}, f32[4,1024]{1,0:T(4,128)S(1)}, u32[]{:S(2)}, u32[]{:S(2)}) %collective-permute-start.14) | collective-permute-done | bytes 16416 | tf_op jit(solution)/shard_map/taps1/ppermute | solution.py:159
  110.3 2.7 %collective-permute-done.13.refs_3_ = bf16[128,1024]{1,0:T(8,128)(2,1)S(1)} collective-permute-done((bf16[128,1024]{1,0:T(8,128)(2,1)S(1)}, bf16[128,1024]{1,0:T(8,128)(2,1)S(1)}, u32[]{:S(2)}, u32[]{:S(2)}) %collective-permute-start.13) | collective-permute-done | bytes 262176 | tf_op jit(solution)/shard_map/step2/ppermute | solution.py:33
  113.0 3.4 %keep.1 = bf16[512,1024]{1,0:T(8,128)(2,1)} custom-call(bf16[512,1024]{1,0:T(8,128)(2,1)} %bitcast.22.value_ref), custom_call_target="tpu_custom_call" | custom-call | tf_op jit(solution)/shard_map/convmove/keep/pallas_call | solution.py:131
  123.6 6.7 %merge.3.refs_2_.refs_1_.refs_0_.part_ref = f32[1024,1024]{1,0:T(8,128)S(1)} custom-call(bf16[4,1024,480]{2,1,0:T(8,128)(2,1)S(1)} %copy-done.5, bf16[480,1024]{1,0:T(8,128)(2,1)S(1)} %copy-done.7, bf16[480,1024]{1,0:T(8,128)(2,1)S(1)} %collective-permute-done.6.refs_1_, bf16[480,1024]{1,0:T(8,128)(2,1)S(1)} %collective-permute-done.7.refs_2_, ...), custom_call_target="tpu_custom_call" | custom-call | tf_op jit(solution)/shard_map/merge/pallas_call | solution.py:317
  130.7 4.4 %collective-permute-start.19 = (bf16[192,1024]{1,0:T(8,128)(2,1)S(1)}, bf16[192,1024]{1,0:T(8,128)(2,1)S(1)}, u32[]{:S(2)}, u32[]{:S(2)}) collective-permute-start(bf16[192,1024]{1,0:T(8,128)(2,1)S(1)} %get-tuple-element.99), channel_id=1, source_target_pairs={{0,224},{4,228},{8,232},{12,236},{16,240},{20,244},{24,248},{28,25... | collective-permute-start | bytes 1179656 | tf_op jit(solution)/shard_map/step4/ppermute | solution.py:33
  135.2 8.1 %collective-permute-done.20 = f32[4,1024]{1,0:T(4,128)S(1)} collective-permute-done((f32[4,1024]{1,0:T(4,128)S(1)}, f32[4,1024]{1,0:T(4,128)S(1)}, u32[]{:S(2)}, u32[]{:S(2)}) %collective-permute-start.20) | collective-permute-done | bytes 16416 | tf_op jit(solution)/shard_map/taps3/ppermute | solution.py:159
  143.3 3.0 %collective-permute-done.18.refs_3_ = bf16[192,1024]{1,0:T(8,128)(2,1)S(1)} collective-permute-done((bf16[192,1024]{1,0:T(8,128)(2,1)S(1)}, bf16[192,1024]{1,0:T(8,128)(2,1)S(1)}, u32[]{:S(2)}, u32[]{:S(2)}) %collective-permute-start.18) | collective-permute-done | bytes 393248 | tf_op jit(solution)/shard_map/step4/ppermute | solution.py:33
  149.7 2.9 %collective-permute-done.23 = f32[4,1024]{1,0:T(4,128)S(1)} collective-permute-done((f32[4,1024]{1,0:T(4,128)S(1)}, f32[4,1024]{1,0:T(4,128)S(1)}, u32[]{:S(2)}, u32[]{:S(2)}) %collective-permute-start.23) | collective-permute-done | bytes 16416 | tf_op jit(solution)/shard_map/taps4/ppermute | solution.py:159
  158.9 4.2 %collective-permute-done.26 = f32[4,1024]{1,0:T(4,128)S(1)} collective-permute-done((f32[4,1024]{1,0:T(4,128)S(1)}, f32[4,1024]{1,0:T(4,128)S(1)}, u32[]{:S(2)}, u32[]{:S(2)}) %collective-permute-start.26) | collective-permute-done | bytes 16416 | tf_op jit(solution)/shard_map/taps5/ppermute | solution.py:159
  166.1 4.3 %collective-permute-done.28.back_ref = bf16[128,1024]{1,0:T(8,128)(2,1)S(1)} collective-permute-done((bf16[128,1024]{1,0:T(8,128)(2,1)S(1)}, bf16[128,1024]{1,0:T(8,128)(2,1)S(1)}, u32[]{:S(2)}, u32[]{:S(2)}) %collective-permute-start.28) | collective-permute-done | bytes 262176 | tf_op jit(solution)/shard_map/step7/ppermute | solution.py:33
  (118 shorter events, 60.8 us)
Async XLA Ops:
  9.8 13.0 %collective-permute-start.2 = (bf16[960,2048]{1,0:T(8,128)(2,1)S(1)}, bf16[960,2048]{1,0:T(8,128)(2,1)S(1)}, u32[]{:S(2)}, u32[]{:S(2)}) collective-permute-start(bf16[960,2048]{1,0:T(8,128)(2,1)S(1)} %fusion.4), channel_id=1, source_target_pairs={{0,4},{4,0},{8,12},{12,8},{16,20},{20,16},{24,28},{28,24},{32,36},... | collective-permute-start | bytes 11796488 | tf_op jit(solution)/shard_map/swap/ppermute | solution.py:33
  9.9 12.8 %collective-permute-start = (bf16[3,4096]{1,0:T(4,128)(2,1)S(1)}, bf16[3,4096]{1,0:T(4,128)(2,1)S(1)}, u32[]{:S(2)}, u32[]{:S(2)}) collective-permute-start(bf16[3,4096]{1,0:T(4,128)(2,1)S(1)} %get-tuple-element.114), channel_id=1, source_target_pairs={{0,1},{1,2},{2,3},{3,4},{4,5},{5,6},{6,7},{7,8},{8,9},{9,10},{10,1... | collective-permute-start | bytes 73736 | tf_op jit(solution)/shard_map/convedges/ppermute | solution.py:43
  28.3 52.9 %collective-permute-start.3 = (bf16[480,1024]{1,0:T(8,128)(2,1)}, bf16[480,1024]{1,0:T(8,128)(2,1)}, u32[]{:S(2)}, u32[]{:S(2)}) collective-permute-start(bf16[480,1024]{1,0:T(8,128)(2,1)} %get-tuple-element.62), channel_id=1, source_target_pairs={{0,8},{4,12},{8,16},{12,20},{16,24},{20,28},{24,0},{28,4},{32,40},... | collective-permute-start | bytes 2949128 | tf_op jit(solution)/shard_map/rows0/ppermute | solution.py:33
  29.6 51.6 %collective-permute-start.5 = (bf16[480,1024]{1,0:T(8,128)(2,1)}, bf16[480,1024]{1,0:T(8,128)(2,1)}, u32[]{:S(2)}, u32[]{:S(2)}) collective-permute-start(bf16[480,1024]{1,0:T(8,128)(2,1)} %get-tuple-element.63), channel_id=1, source_target_pairs={{0,16},{4,20},{8,24},{12,28},{16,0},{20,4},{24,8},{28,12},{32,48},... | collective-permute-start | bytes 2949128 | tf_op jit(solution)/shard_map/rows0/ppermute | solution.py:33
  32.5 48.7 %collective-permute-start.4 = (bf16[480,1024]{1,0:T(8,128)(2,1)}, bf16[480,1024]{1,0:T(8,128)(2,1)}, u32[]{:S(2)}, u32[]{:S(2)}) collective-permute-start(bf16[480,1024]{1,0:T(8,128)(2,1)} %get-tuple-element.64), channel_id=1, source_target_pairs={{0,24},{4,28},{8,0},{12,4},{16,8},{20,12},{24,16},{28,20},{32,56},... | collective-permute-start | bytes 2949128 | tf_op jit(solution)/shard_map/rows0/ppermute | solution.py:33
  34.5 9.1 %all-to-all-start.1 = ((f32[4,4,1024]{2,1,0:T(4,128)}), f32[4,4,1024]{2,1,0:T(4,128)S(1)}, u32[]{:S(2)}, u32[]{:S(2)}) async-start(f32[4,4,1024]{2,1,0:T(4,128)} %broadcast_in_dim.5), calls=%async_computation.1 | async-start | bytes 131072 | tf_op jit(solution)/shard_map/convtaps/all_to_all | solution.py:102
  43.6 17.9 %all-to-all-start = ((f32[8,20,128]{2,1,0:T(8,128)}), f32[8,20,128]{2,1,0:T(8,128)S(1)}, u32[]{:S(2)}, u32[]{:S(2)}) async-start(f32[8,20,128]{2,1,0:T(8,128)} %broadcast_in_dim.4), calls=%async_computation | async-start | bytes 196608 | tf_op jit(solution)/shard_map/info/all_to_all | solution.py:520
  62.2 14.2 %all-to-all-start.2 = ((f32[4,4,1024]{2,1,0:T(4,128)}), f32[4,4,1024]{2,1,0:T(4,128)S(1)}, u32[]{:S(2)}, u32[]{:S(2)}) async-start(f32[4,4,1024]{2,1,0:T(4,128)} %pad_maximum_fusion.4), calls=%async_computation.2 | async-start | bytes 131072 | tf_op jit(solution)/shard_map/tapsmove/all_to_all | solution.py:118
  76.4 36.6 %all-to-all-start.3 = ((bf16[128,4,1024]{2,0,1:T(8,128)(2,1)}), bf16[128,4,1024]{2,0,1:T(8,128)(2,1)}, u32[]{:S(2)}, u32[]{:S(2)}) async-start(bf16[128,4,1024]{2,0,1:T(8,128)(2,1)} %bitcast.51), calls=%async_computation.3 | async-start | bytes 2097152 | tf_op jit(solution)/shard_map/convmove/all_to_all | solution.py:128
  81.2 41.8 %collective-permute-start.6 = (bf16[480,1024]{1,0:T(8,128)(2,1)}, bf16[480,1024]{1,0:T(8,128)(2,1)S(1)}, u32[]{:S(2)}, u32[]{:S(2)}) collective-permute-start(bf16[480,1024]{1,0:T(8,128)(2,1)} %get-tuple-element.82), channel_id=1, source_target_pairs={{0,8},{4,12},{8,16},{12,20},{16,24},{20,28},{24,0},{28,4},{32,40},... | collective-permute-start | bytes 2949128 | tf_op jit(solution)/shard_map/rows1/ppermute | solution.py:33
  82.4 40.7 %collective-permute-start.7 = (bf16[480,1024]{1,0:T(8,128)(2,1)}, bf16[480,1024]{1,0:T(8,128)(2,1)S(1)}, u32[]{:S(2)}, u32[]{:S(2)}) collective-permute-start(bf16[480,1024]{1,0:T(8,128)(2,1)} %get-tuple-element.83), channel_id=1, source_target_pairs={{0,24},{4,28},{8,0},{12,4},{16,8},{20,12},{24,16},{28,20},{32,56},... | collective-permute-start | bytes 2949128 | tf_op jit(solution)/shard_map/rows1/ppermute | solution.py:33
  84.7 38.9 %collective-permute-start.8 = (bf16[480,1024]{1,0:T(8,128)(2,1)}, bf16[480,1024]{1,0:T(8,128)(2,1)}, u32[]{:S(2)}, u32[]{:S(2)}) collective-permute-start(bf16[480,1024]{1,0:T(8,128)(2,1)} %get-tuple-element.84), channel_id=1, source_target_pairs={{0,16},{4,20},{8,24},{12,28},{16,0},{20,4},{24,8},{28,12},{32,48},... | collective-permute-start | bytes 2949128 | tf_op jit(solution)/shard_map/rows1/ppermute | solution.py:33
  86.5 9.6 %collective-permute-start.11 = (f32[4,1024]{1,0:T(4,128)S(1)}, f32[4,1024]{1,0:T(4,128)S(1)}, u32[]{:S(2)}, u32[]{:S(2)}) collective-permute-start(f32[4,1024]{1,0:T(4,128)S(1)} %broadcast_multiply_fusion), channel_id=1, source_target_pairs={{0,4},{4,0},{8,12},{12,8},{16,20},{20,16},{24,28},{28,24},{32,36},... | collective-permute-start | bytes 49160 | tf_op jit(solution)/shard_map/taps0/ppermute | solution.py:159
  96.1 8.9 %collective-permute-start.10 = (bf16[64,1024]{1,0:T(8,128)(2,1)S(1)}, bf16[64,1024]{1,0:T(8,128)(2,1)S(1)}, u32[]{:S(2)}, u32[]{:S(2)}) collective-permute-start(bf16[64,1024]{1,0:T(8,128)(2,1)S(1)} %get-tuple-element.86), channel_id=1, source_target_pairs={{0,224},{4,228},{8,232},{12,236},{16,240},{20,244},{24,248},{28,25... | collective-permute-start | bytes 393224 | tf_op jit(solution)/shard_map/step1/ppermute | solution.py:33
  105.3 7.7 %collective-permute-start.13 = (bf16[128,1024]{1,0:T(8,128)(2,1)S(1)}, bf16[128,1024]{1,0:T(8,128)(2,1)S(1)}, u32[]{:S(2)}, u32[]{:S(2)}) collective-permute-start(bf16[128,1024]{1,0:T(8,128)(2,1)S(1)} %get-tuple-element.90), channel_id=1, source_target_pairs={{0,224},{4,228},{8,232},{12,236},{16,240},{20,244},{24,248},{28,25... | collective-permute-start | bytes 786440 | tf_op jit(solution)/shard_map/step2/ppermute | solution.py:33
  110.3 8.2 %collective-permute-start.12 = (bf16[128,1024]{1,0:T(8,128)(2,1)S(1)}, bf16[128,1024]{1,0:T(8,128)(2,1)S(1)}, u32[]{:S(2)}, u32[]{:S(2)}) collective-permute-start(bf16[128,1024]{1,0:T(8,128)(2,1)S(1)} %get-tuple-element.88), channel_id=1, source_target_pairs={{0,32},{4,36},{8,40},{12,44},{16,48},{20,52},{24,56},{28,60},{32,6... | collective-permute-start | bytes 786440 | tf_op jit(solution)/shard_map/step2/ppermute | solution.py:33
  113.0 8.3 %collective-permute-start.17 = (f32[4,1024]{1,0:T(4,128)S(1)}, f32[4,1024]{1,0:T(4,128)S(1)}, u32[]{:S(2)}, u32[]{:S(2)}) collective-permute-start(f32[4,1024]{1,0:T(4,128)S(1)} %add.89), channel_id=1, source_target_pairs={{0,64},{4,68},{8,72},{12,76},{16,80},{20,84},{24,88},{28,92},{32,9... | collective-permute-start | bytes 49160 | tf_op jit(solution)/shard_map/taps2/ppermute | solution.py:159
  120.9 9.4 %collective-permute-start.16 = (bf16[128,1024]{1,0:T(8,128)(2,1)S(1)}, bf16[128,1024]{1,0:T(8,128)(2,1)S(1)}, u32[]{:S(2)}, u32[]{:S(2)}) collective-permute-start(bf16[128,1024]{1,0:T(8,128)(2,1)S(1)} %get-tuple-element.95), channel_id=1, source_target_pairs={{0,224},{4,228},{8,232},{12,236},{16,240},{20,244},{24,248},{28,25... | collective-permute-start | bytes 786440 | tf_op jit(solution)/shard_map/step3/ppermute | solution.py:33
  121.3 9.0 %collective-permute-start.15 = (bf16[128,1024]{1,0:T(8,128)(2,1)S(1)}, bf16[128,1024]{1,0:T(8,128)(2,1)S(1)}, u32[]{:S(2)}, u32[]{:S(2)}) collective-permute-start(bf16[128,1024]{1,0:T(8,128)(2,1)S(1)} %get-tuple-element.93), channel_id=1, source_target_pairs={{0,32},{4,36},{8,40},{12,44},{16,48},{20,52},{24,56},{28,60},{32,6... | collective-permute-start | bytes 786440 | tf_op jit(solution)/shard_map/step3/ppermute | solution.py:33
  130.7 12.5 %collective-permute-start.19 = (bf16[192,1024]{1,0:T(8,128)(2,1)S(1)}, bf16[192,1024]{1,0:T(8,128)(2,1)S(1)}, u32[]{:S(2)}, u32[]{:S(2)}) collective-permute-start(bf16[192,1024]{1,0:T(8,128)(2,1)S(1)} %get-tuple-element.99), channel_id=1, source_target_pairs={{0,224},{4,228},{8,232},{12,236},{16,240},{20,244},{24,248},{28,25... | collective-permute-start | bytes 1179656 | tf_op jit(solution)/shard_map/step4/ppermute | solution.py:33
  135.2 11.1 %collective-permute-start.18 = (bf16[192,1024]{1,0:T(8,128)(2,1)S(1)}, bf16[192,1024]{1,0:T(8,128)(2,1)S(1)}, u32[]{:S(2)}, u32[]{:S(2)}) collective-permute-start(bf16[192,1024]{1,0:T(8,128)(2,1)S(1)} %get-tuple-element.97), channel_id=1, source_target_pairs={{0,32},{4,36},{8,40},{12,44},{16,48},{20,52},{24,56},{28,60},{32,6... | collective-permute-start | bytes 1179656 | tf_op jit(solution)/shard_map/step4/ppermute | solution.py:33
  135.2 8.1 %collective-permute-start.20 = (f32[4,1024]{1,0:T(4,128)S(1)}, f32[4,1024]{1,0:T(4,128)S(1)}, u32[]{:S(2)}, u32[]{:S(2)}) collective-permute-start(f32[4,1024]{1,0:T(4,128)S(1)} %add.90), channel_id=1, source_target_pairs={{0,32},{4,36},{8,40},{12,44},{16,48},{20,52},{24,56},{28,60},{32,0... | collective-permute-start | bytes 49160 | tf_op jit(solution)/shard_map/taps3/ppermute | solution.py:159
  155.7 8.0 %collective-permute-start.25 = (bf16[128,1024]{1,0:T(8,128)(2,1)S(1)}, bf16[128,1024]{1,0:T(8,128)(2,1)S(1)}, u32[]{:S(2)}, u32[]{:S(2)}) collective-permute-start(bf16[128,1024]{1,0:T(8,128)(2,1)S(1)} %get-tuple-element.108), channel_id=1, source_target_pairs={{0,224},{4,228},{8,232},{12,236},{16,240},{20,244},{24,248},{28,25... | collective-permute-start | bytes 786440 | tf_op jit(solution)/shard_map/step6/ppermute | solution.py:33
  155.8 7.9 %collective-permute-start.24 = (bf16[128,1024]{1,0:T(8,128)(2,1)S(1)}, bf16[128,1024]{1,0:T(8,128)(2,1)S(1)}, u32[]{:S(2)}, u32[]{:S(2)}) collective-permute-start(bf16[128,1024]{1,0:T(8,128)(2,1)S(1)} %get-tuple-element.106), channel_id=1, source_target_pairs={{0,32},{4,36},{8,40},{12,44},{16,48},{20,52},{24,56},{28,60},{32,6... | collective-permute-start | bytes 786440 | tf_op jit(solution)/shard_map/step6/ppermute | solution.py:33
  (24 other events, 142.2 us)

commit v3 on v2

--- a/solution.py
+++ b/solution.py
@@ -461,7 +461,7 @@
 
 
 def holds(input_grad, taps_at):
-    moved = {step: [taps_at[step - 1]] for step in (4, 5, 6, 7)}
+    moved = {step: [taps_at[step - 1]] for step in (4, 5, 6)}
     return {2: [taps_at[1]], 3: [taps_at[2], input_grad]} | moved
 
 

time: 175 us -> 176 us (level)
  no operation moved by 1% of the time
where the time goes in v3:
time: 176 us; the launch traced here: 175 us
  starting transfers between devices  64.1 us (36%)
  waiting for transfers between devices  45.5 us (26%)
  Pallas kernels  36.5 us (21%)
  local copies, waits for them, and re-layouts  14.2 us (8%)
  matrix products  10.2 us (6%)
  other arithmetic  3.28 us (2%)
    ppermute x21, starting transfers between devices, shift(): return lax.ppermute(value, 'expert', pairs)  28.9 us
    ppermute x21, waiting for transfers between devices, shift(): return lax.ppermute(value, 'expert', pairs)  21.1 us
    ppermute x6, waiting for transfers between devices, flip_sum(): return value + lax.ppermute(value, 'expert', pairs)  19.5 us
    pallas_call x2, Pallas kernels, merge_rows(): pl.pallas_call(merge_kernel, grid=(columns // tile,), in_specs=[pl.BlockS...  13.3 us
    unnamed x30, local copies, waits for them, and re-layouts  10.7 us
    all_to_all x1, starting transfers between devices, expert_part(): lax.all_to_all(column, 'expert', split_axis=0, concat_axis=0, tiled=True,...  9.2 us
    pallas_call x2, Pallas kernels, pack(): pl.pallas_call(pack_kernel, grid=(columns // tile,), in_specs=[pl.BlockSp...  7.17 us
    ppermute x2, starting transfers between devices, from_behind(): lax.ppermute(value, axis, [(source, source + steps) for source in range(l...  6.13 us
  transfers between devices with their start and end apart: 33, of which 15 were waited for; matrix products, arithmetic and copies ran while one was open for 7% of the time, Pallas kernels for 16%

profile of v3, /device:TPU:6, one launch (start us, length us, event | category | flops | bytes accessed | tf_op | source)
XLA Modules:
  0.0 174.9 jit_solution(11089887564719700320)
XLA Ops:
  5.3 4.5 %fusion.4 = bf16[960,2048]{1,0:T(8,128)(2,1)S(1)} fusion(bf16[960,1024]{1,0:T(8,128)(2,1)S(1)} %bitcast.55, bf16[1,1024,2048]{2,1,0:T(8,128)(2,1)S(1)} %copy-done.14), kind=kOutput, calls=%fused_computation.4 | convolution fusion | flops 4028497920 | bytes 10092544 | tf_op jit(solution)/shard_map/multiply/dot_general | solution.py:492
  9.9 4.2 %collective-permute-start = (bf16[3,4096]{1,0:T(4,128)(2,1)S(1)}, bf16[3,4096]{1,0:T(4,128)(2,1)S(1)}, u32[]{:S(2)}, u32[]{:S(2)}) collective-permute-start(bf16[3,4096]{1,0:T(4,128)(2,1)S(1)} %get-tuple-element.110), channel_id=1, source_target_pairs={{0,1},{1,2},{2,3},{3,4},{4,5},{5,6},{6,7},{7,8},{8,9},{9,10},{10,1... | collective-permute-start | bytes 73736 | tf_op jit(solution)/shard_map/convedges/ppermute | solution.py:43
  17.0 5.7 %fusion.7.kept_ref = bf16[960,2048]{1,0:T(8,128)(2,1)} fusion(bf16[1,1024,2048]{2,1,0:T(8,128)(2,1)S(1)} %copy-done.14, bf16[1920,1024]{1,0:T(8,128)(2,1)S(1)} %bitcast.52), kind=kOutput, calls=%fused_computation.5 | convolution fusion | flops 4028497920 | bytes 10092544 | tf_op jit(solution)/shard_map/multiply/dot_general | solution.py:494
  24.8 3.6 %pack.2 = (bf16[480,1024]{1,0:T(8,128)(2,1)}, bf16[480,1024]{1,0:T(8,128)(2,1)}, bf16[480,1024]{1,0:T(8,128)(2,1)}, bf16[480,1024]{1,0:T(8,128)(2,1)}) custom-call(bf16[960,2048]{1,0:T(8,128)(2,1)} %fusion.7.kept_ref, bf16[960,2048]{1,0:T(8,128)(2,1)} %copy-done.9), custom_call_target="tpu_custom_call" | custom-call | bytes 7864320 | tf_op jit(solution)/shard_map/pack0/pack/pallas_call | solution.py:292
  29.6 2.9 %collective-permute-start.5 = (bf16[480,1024]{1,0:T(8,128)(2,1)}, bf16[480,1024]{1,0:T(8,128)(2,1)}, u32[]{:S(2)}, u32[]{:S(2)}) collective-permute-start(bf16[480,1024]{1,0:T(8,128)(2,1)} %get-tuple-element.61), channel_id=1, source_target_pairs={{0,16},{4,20},{8,24},{12,28},{16,0},{20,4},{24,8},{28,12},{32,48},... | collective-permute-start | bytes 2949128 | tf_op jit(solution)/shard_map/rows0/ppermute | solution.py:33
  34.5 5.6 %all-to-all-start.1 = ((f32[4,4,1024]{2,1,0:T(4,128)}), f32[4,4,1024]{2,1,0:T(4,128)S(1)}, u32[]{:S(2)}, u32[]{:S(2)}) async-start(f32[4,4,1024]{2,1,0:T(4,128)} %broadcast_in_dim.5), calls=%async_computation.1 | async-start | bytes 131072 | tf_op jit(solution)/shard_map/convtaps/all_to_all | solution.py:102
  43.6 9.2 %all-to-all-start = ((f32[8,20,128]{2,1,0:T(8,128)}), f32[8,20,128]{2,1,0:T(8,128)S(1)}, u32[]{:S(2)}, u32[]{:S(2)}) async-start(f32[8,20,128]{2,1,0:T(8,128)} %broadcast_in_dim.4), calls=%async_computation | async-start | bytes 196608 | tf_op jit(solution)/shard_map/info/all_to_all | solution.py:520
  52.9 5.1 %conv.1 = (bf16[128,4096]{1,0:T(8,128)(2,1)S(1)}, f32[4,4096]{1,0:T(4,128)S(1)}) custom-call(bf16[131,4096]{1,0:T(8,128)(2,1)S(1)} %pad_maximum_fusion.grad_ref, bf16[134,4096]{1,0:T(8,128)(2,1)S(1)} %pad_maximum_fusion.1.input_ref, f32[4,4096]{1,0:T(4,128)S(1)} %pad_maximum_fusion.3.taps_ref), custom_call_target="tpu_custom_call" | custom-call | bytes 12000000 | tf_op jit(solution)/shard_map/convcore/conv/pallas_call | solution.py:72
  58.0 3.6 %all-to-all-done.info_ref = f32[8,20,128]{2,1,0:T(8,128)S(1)} async-done(((f32[8,20,128]{2,1,0:T(8,128)}), f32[8,20,128]{2,1,0:T(8,128)S(1)}, u32[]{:S(2)}, u32[]{:S(2)}) %all-to-all-start) | async-done | bytes 81952 | tf_op jit(solution)/shard_map/info/all_to_all | solution.py:520
  62.2 5.3 %all-to-all-start.2 = ((f32[4,4,1024]{2,1,0:T(4,128)}), f32[4,4,1024]{2,1,0:T(4,128)S(1)}, u32[]{:S(2)}, u32[]{:S(2)}) async-start(f32[4,4,1024]{2,1,0:T(4,128)} %pad_maximum_fusion.4), calls=%async_computation.2 | async-start | bytes 131072 | tf_op jit(solution)/shard_map/tapsmove/all_to_all | solution.py:118
  67.5 3.6 %pack.3 = (bf16[480,1024]{1,0:T(8,128)(2,1)}, bf16[480,1024]{1,0:T(8,128)(2,1)}, bf16[480,1024]{1,0:T(8,128)(2,1)}, bf16[480,1024]{1,0:T(8,128)(2,1)}) custom-call(bf16[960,2048]{1,0:T(8,128)(2,1)} %fusion.7.kept_ref, bf16[960,2048]{1,0:T(8,128)(2,1)} %copy-done.9), custom_call_target="tpu_custom_call" | custom-call | bytes 7864320 | tf_op jit(solution)/shard_map/pack1/pack/pallas_call | solution.py:292
  76.4 4.8 %all-to-all-start.3 = ((bf16[128,4,1024]{2,0,1:T(8,128)(2,1)}), bf16[128,4,1024]{2,0,1:T(8,128)(2,1)}, u32[]{:S(2)}, u32[]{:S(2)}) async-start(bf16[128,4,1024]{2,0,1:T(8,128)(2,1)} %bitcast.51), calls=%async_computation.3 | async-start | bytes 2097152 | tf_op jit(solution)/shard_map/convmove/all_to_all | solution.py:128
  88.6 6.6 %merge.2.refs_0_.refs_1_ = f32[1024,1024]{1,0:T(8,128)S(1)} custom-call(bf16[4,1024,480]{2,1,0:T(8,128)(2,1)S(1)} %copy-done.4, bf16[480,1024]{1,0:T(8,128)(2,1)S(1)} %copy-done.8, bf16[480,1024]{1,0:T(8,128)(2,1)} %collective-permute-done.3.refs_1_, bf16[480,1024]{1,0:T(8,128)(2,1)} %collective-permute-done.4.refs_2_, ...), custom_call_target="tpu_custom_call" | custom-call | tf_op jit(solution)/shard_map/merge/pallas_call | solution.py:317
  98.8 3.9 %collective-permute-done.9.refs_2_ = bf16[64,1024]{1,0:T(8,128)(2,1)S(1)} collective-permute-done((bf16[64,1024]{1,0:T(8,128)(2,1)S(1)}, bf16[64,1024]{1,0:T(8,128)(2,1)S(1)}, u32[]{:S(2)}, u32[]{:S(2)}) %collective-permute-start.9) | collective-permute-done | bytes 131104 | tf_op jit(solution)/shard_map/step1/ppermute | solution.py:33
  105.9 4.3 %collective-permute-done.14 = f32[4,1024]{1,0:T(4,128)S(1)} collective-permute-done((f32[4,1024]{1,0:T(4,128)S(1)}, f32[4,1024]{1,0:T(4,128)S(1)}, u32[]{:S(2)}, u32[]{:S(2)}) %collective-permute-start.14) | collective-permute-done | bytes 16416 | tf_op jit(solution)/shard_map/taps1/ppermute | solution.py:159
  110.3 2.7 %collective-permute-done.13.refs_3_ = bf16[128,1024]{1,0:T(8,128)(2,1)S(1)} collective-permute-done((bf16[128,1024]{1,0:T(8,128)(2,1)S(1)}, bf16[128,1024]{1,0:T(8,128)(2,1)S(1)}, u32[]{:S(2)}, u32[]{:S(2)}) %collective-permute-start.13) | collective-permute-done | bytes 262176 | tf_op jit(solution)/shard_map/step2/ppermute | solution.py:33
  113.0 3.4 %keep.1 = bf16[512,1024]{1,0:T(8,128)(2,1)} custom-call(bf16[512,1024]{1,0:T(8,128)(2,1)} %bitcast.22.value_ref), custom_call_target="tpu_custom_call" | custom-call | tf_op jit(solution)/shard_map/convmove/keep/pallas_call | solution.py:131
  123.6 6.7 %merge.3.refs_2_.refs_1_.refs_0_.part_ref = f32[1024,1024]{1,0:T(8,128)S(1)} custom-call(bf16[4,1024,480]{2,1,0:T(8,128)(2,1)S(1)} %copy-done.5, bf16[480,1024]{1,0:T(8,128)(2,1)S(1)} %copy-done.7, bf16[480,1024]{1,0:T(8,128)(2,1)S(1)} %collective-permute-done.6.refs_1_, bf16[480,1024]{1,0:T(8,128)(2,1)S(1)} %collective-permute-done.7.refs_2_, ...), custom_call_target="tpu_custom_call" | custom-call | tf_op jit(solution)/shard_map/merge/pallas_call | solution.py:317
  130.7 4.4 %collective-permute-start.19 = (bf16[192,1024]{1,0:T(8,128)(2,1)S(1)}, bf16[192,1024]{1,0:T(8,128)(2,1)S(1)}, u32[]{:S(2)}, u32[]{:S(2)}) collective-permute-start(bf16[192,1024]{1,0:T(8,128)(2,1)S(1)} %get-tuple-element.97), channel_id=1, source_target_pairs={{0,224},{4,228},{8,232},{12,236},{16,240},{20,244},{24,248},{28,25... | collective-permute-start | bytes 1179656 | tf_op jit(solution)/shard_map/step4/ppermute | solution.py:33
  135.2 8.1 %collective-permute-done.20 = f32[4,1024]{1,0:T(4,128)S(1)} collective-permute-done((f32[4,1024]{1,0:T(4,128)S(1)}, f32[4,1024]{1,0:T(4,128)S(1)}, u32[]{:S(2)}, u32[]{:S(2)}) %collective-permute-start.20) | collective-permute-done | bytes 16416 | tf_op jit(solution)/shard_map/taps3/ppermute | solution.py:159
  143.3 3.0 %collective-permute-done.18.refs_3_ = bf16[192,1024]{1,0:T(8,128)(2,1)S(1)} collective-permute-done((bf16[192,1024]{1,0:T(8,128)(2,1)S(1)}, bf16[192,1024]{1,0:T(8,128)(2,1)S(1)}, u32[]{:S(2)}, u32[]{:S(2)}) %collective-permute-start.18) | collective-permute-done | bytes 393248 | tf_op jit(solution)/shard_map/step4/ppermute | solution.py:33
  149.7 2.9 %collective-permute-done.23 = f32[4,1024]{1,0:T(4,128)S(1)} collective-permute-done((f32[4,1024]{1,0:T(4,128)S(1)}, f32[4,1024]{1,0:T(4,128)S(1)}, u32[]{:S(2)}, u32[]{:S(2)}) %collective-permute-start.23) | collective-permute-done | bytes 16416 | tf_op jit(solution)/shard_map/taps4/ppermute | solution.py:159
  157.8 4.3 %collective-permute-done.25.refs_3_ = bf16[128,1024]{1,0:T(8,128)(2,1)S(1)} collective-permute-done((bf16[128,1024]{1,0:T(8,128)(2,1)S(1)}, bf16[128,1024]{1,0:T(8,128)(2,1)S(1)}, u32[]{:S(2)}, u32[]{:S(2)}) %collective-permute-start.25) | collective-permute-done | bytes 262176 | tf_op jit(solution)/shard_map/step6/ppermute | solution.py:33
  168.5 4.2 %collective-permute-done.28 = f32[4,1024]{1,0:T(4,128)S(1)} collective-permute-done((f32[4,1024]{1,0:T(4,128)S(1)}, f32[4,1024]{1,0:T(4,128)S(1)}, u32[]{:S(2)}, u32[]{:S(2)}) %collective-permute-start.28) | collective-permute-done | bytes 16416 | tf_op jit(solution)/shard_map/taps5/ppermute | solution.py:159
  (118 shorter events, 61.1 us)
Async XLA Ops:
  9.8 13.0 %collective-permute-start.2 = (bf16[960,2048]{1,0:T(8,128)(2,1)S(1)}, bf16[960,2048]{1,0:T(8,128)(2,1)S(1)}, u32[]{:S(2)}, u32[]{:S(2)}) collective-permute-start(bf16[960,2048]{1,0:T(8,128)(2,1)S(1)} %fusion.4), channel_id=1, source_target_pairs={{0,4},{4,0},{8,12},{12,8},{16,20},{20,16},{24,28},{28,24},{32,36},... | collective-permute-start | bytes 11796488 | tf_op jit(solution)/shard_map/swap/ppermute | solution.py:33
  9.9 12.8 %collective-permute-start = (bf16[3,4096]{1,0:T(4,128)(2,1)S(1)}, bf16[3,4096]{1,0:T(4,128)(2,1)S(1)}, u32[]{:S(2)}, u32[]{:S(2)}) collective-permute-start(bf16[3,4096]{1,0:T(4,128)(2,1)S(1)} %get-tuple-element.110), channel_id=1, source_target_pairs={{0,1},{1,2},{2,3},{3,4},{4,5},{5,6},{6,7},{7,8},{8,9},{9,10},{10,1... | collective-permute-start | bytes 73736 | tf_op jit(solution)/shard_map/convedges/ppermute | solution.py:43
  28.3 52.9 %collective-permute-start.3 = (bf16[480,1024]{1,0:T(8,128)(2,1)}, bf16[480,1024]{1,0:T(8,128)(2,1)}, u32[]{:S(2)}, u32[]{:S(2)}) collective-permute-start(bf16[480,1024]{1,0:T(8,128)(2,1)} %get-tuple-element.60), channel_id=1, source_target_pairs={{0,8},{4,12},{8,16},{12,20},{16,24},{20,28},{24,0},{28,4},{32,40},... | collective-permute-start | bytes 2949128 | tf_op jit(solution)/shard_map/rows0/ppermute | solution.py:33
  29.6 51.6 %collective-permute-start.5 = (bf16[480,1024]{1,0:T(8,128)(2,1)}, bf16[480,1024]{1,0:T(8,128)(2,1)}, u32[]{:S(2)}, u32[]{:S(2)}) collective-permute-start(bf16[480,1024]{1,0:T(8,128)(2,1)} %get-tuple-element.61), channel_id=1, source_target_pairs={{0,16},{4,20},{8,24},{12,28},{16,0},{20,4},{24,8},{28,12},{32,48},... | collective-permute-start | bytes 2949128 | tf_op jit(solution)/shard_map/rows0/ppermute | solution.py:33
  32.5 48.7 %collective-permute-start.4 = (bf16[480,1024]{1,0:T(8,128)(2,1)}, bf16[480,1024]{1,0:T(8,128)(2,1)}, u32[]{:S(2)}, u32[]{:S(2)}) collective-permute-start(bf16[480,1024]{1,0:T(8,128)(2,1)} %get-tuple-element.62), channel_id=1, source_target_pairs={{0,24},{4,28},{8,0},{12,4},{16,8},{20,12},{24,16},{28,20},{32,56},... | collective-permute-start | bytes 2949128 | tf_op jit(solution)/shard_map/rows0/ppermute | solution.py:33
  34.5 9.1 %all-to-all-start.1 = ((f32[4,4,1024]{2,1,0:T(4,128)}), f32[4,4,1024]{2,1,0:T(4,128)S(1)}, u32[]{:S(2)}, u32[]{:S(2)}) async-start(f32[4,4,1024]{2,1,0:T(4,128)} %broadcast_in_dim.5), calls=%async_computation.1 | async-start | bytes 131072 | tf_op jit(solution)/shard_map/convtaps/all_to_all | solution.py:102
  43.6 17.9 %all-to-all-start = ((f32[8,20,128]{2,1,0:T(8,128)}), f32[8,20,128]{2,1,0:T(8,128)S(1)}, u32[]{:S(2)}, u32[]{:S(2)}) async-start(f32[8,20,128]{2,1,0:T(8,128)} %broadcast_in_dim.4), calls=%async_computation | async-start | bytes 196608 | tf_op jit(solution)/shard_map/info/all_to_all | solution.py:520
  62.2 14.2 %all-to-all-start.2 = ((f32[4,4,1024]{2,1,0:T(4,128)}), f32[4,4,1024]{2,1,0:T(4,128)S(1)}, u32[]{:S(2)}, u32[]{:S(2)}) async-start(f32[4,4,1024]{2,1,0:T(4,128)} %pad_maximum_fusion.4), calls=%async_computation.2 | async-start | bytes 131072 | tf_op jit(solution)/shard_map/tapsmove/all_to_all | solution.py:118
  76.4 36.6 %all-to-all-start.3 = ((bf16[128,4,1024]{2,0,1:T(8,128)(2,1)}), bf16[128,4,1024]{2,0,1:T(8,128)(2,1)}, u32[]{:S(2)}, u32[]{:S(2)}) async-start(bf16[128,4,1024]{2,0,1:T(8,128)(2,1)} %bitcast.51), calls=%async_computation.3 | async-start | bytes 2097152 | tf_op jit(solution)/shard_map/convmove/all_to_all | solution.py:128
  81.2 41.8 %collective-permute-start.6 = (bf16[480,1024]{1,0:T(8,128)(2,1)}, bf16[480,1024]{1,0:T(8,128)(2,1)S(1)}, u32[]{:S(2)}, u32[]{:S(2)}) collective-permute-start(bf16[480,1024]{1,0:T(8,128)(2,1)} %get-tuple-element.80), channel_id=1, source_target_pairs={{0,8},{4,12},{8,16},{12,20},{16,24},{20,28},{24,0},{28,4},{32,40},... | collective-permute-start | bytes 2949128 | tf_op jit(solution)/shard_map/rows1/ppermute | solution.py:33
  82.4 40.7 %collective-permute-start.7 = (bf16[480,1024]{1,0:T(8,128)(2,1)}, bf16[480,1024]{1,0:T(8,128)(2,1)S(1)}, u32[]{:S(2)}, u32[]{:S(2)}) collective-permute-start(bf16[480,1024]{1,0:T(8,128)(2,1)} %get-tuple-element.81), channel_id=1, source_target_pairs={{0,24},{4,28},{8,0},{12,4},{16,8},{20,12},{24,16},{28,20},{32,56},... | collective-permute-start | bytes 2949128 | tf_op jit(solution)/shard_map/rows1/ppermute | solution.py:33
  84.7 38.9 %collective-permute-start.8 = (bf16[480,1024]{1,0:T(8,128)(2,1)}, bf16[480,1024]{1,0:T(8,128)(2,1)}, u32[]{:S(2)}, u32[]{:S(2)}) collective-permute-start(bf16[480,1024]{1,0:T(8,128)(2,1)} %get-tuple-element.82), channel_id=1, source_target_pairs={{0,16},{4,20},{8,24},{12,28},{16,0},{20,4},{24,8},{28,12},{32,48},... | collective-permute-start | bytes 2949128 | tf_op jit(solution)/shard_map/rows1/ppermute | solution.py:33
  86.5 9.6 %collective-permute-start.11 = (f32[4,1024]{1,0:T(4,128)S(1)}, f32[4,1024]{1,0:T(4,128)S(1)}, u32[]{:S(2)}, u32[]{:S(2)}) collective-permute-start(f32[4,1024]{1,0:T(4,128)S(1)} %broadcast_multiply_fusion), channel_id=1, source_target_pairs={{0,4},{4,0},{8,12},{12,8},{16,20},{20,16},{24,28},{28,24},{32,36},... | collective-permute-start | bytes 49160 | tf_op jit(solution)/shard_map/taps0/ppermute | solution.py:159
  96.1 8.9 %collective-permute-start.10 = (bf16[64,1024]{1,0:T(8,128)(2,1)S(1)}, bf16[64,1024]{1,0:T(8,128)(2,1)S(1)}, u32[]{:S(2)}, u32[]{:S(2)}) collective-permute-start(bf16[64,1024]{1,0:T(8,128)(2,1)S(1)} %get-tuple-element.84), channel_id=1, source_target_pairs={{0,224},{4,228},{8,232},{12,236},{16,240},{20,244},{24,248},{28,25... | collective-permute-start | bytes 393224 | tf_op jit(solution)/shard_map/step1/ppermute | solution.py:33
  105.3 7.7 %collective-permute-start.13 = (bf16[128,1024]{1,0:T(8,128)(2,1)S(1)}, bf16[128,1024]{1,0:T(8,128)(2,1)S(1)}, u32[]{:S(2)}, u32[]{:S(2)}) collective-permute-start(bf16[128,1024]{1,0:T(8,128)(2,1)S(1)} %get-tuple-element.88), channel_id=1, source_target_pairs={{0,224},{4,228},{8,232},{12,236},{16,240},{20,244},{24,248},{28,25... | collective-permute-start | bytes 786440 | tf_op jit(solution)/shard_map/step2/ppermute | solution.py:33
  110.3 8.2 %collective-permute-start.12 = (bf16[128,1024]{1,0:T(8,128)(2,1)S(1)}, bf16[128,1024]{1,0:T(8,128)(2,1)S(1)}, u32[]{:S(2)}, u32[]{:S(2)}) collective-permute-start(bf16[128,1024]{1,0:T(8,128)(2,1)S(1)} %get-tuple-element.86), channel_id=1, source_target_pairs={{0,32},{4,36},{8,40},{12,44},{16,48},{20,52},{24,56},{28,60},{32,6... | collective-permute-start | bytes 786440 | tf_op jit(solution)/shard_map/step2/ppermute | solution.py:33
  113.0 8.3 %collective-permute-start.17 = (f32[4,1024]{1,0:T(4,128)S(1)}, f32[4,1024]{1,0:T(4,128)S(1)}, u32[]{:S(2)}, u32[]{:S(2)}) collective-permute-start(f32[4,1024]{1,0:T(4,128)S(1)} %add.89), channel_id=1, source_target_pairs={{0,64},{4,68},{8,72},{12,76},{16,80},{20,84},{24,88},{28,92},{32,9... | collective-permute-start | bytes 49160 | tf_op jit(solution)/shard_map/taps2/ppermute | solution.py:159
  120.9 9.4 %collective-permute-start.16 = (bf16[128,1024]{1,0:T(8,128)(2,1)S(1)}, bf16[128,1024]{1,0:T(8,128)(2,1)S(1)}, u32[]{:S(2)}, u32[]{:S(2)}) collective-permute-start(bf16[128,1024]{1,0:T(8,128)(2,1)S(1)} %get-tuple-element.93), channel_id=1, source_target_pairs={{0,224},{4,228},{8,232},{12,236},{16,240},{20,244},{24,248},{28,25... | collective-permute-start | bytes 786440 | tf_op jit(solution)/shard_map/step3/ppermute | solution.py:33
  121.3 9.0 %collective-permute-start.15 = (bf16[128,1024]{1,0:T(8,128)(2,1)S(1)}, bf16[128,1024]{1,0:T(8,128)(2,1)S(1)}, u32[]{:S(2)}, u32[]{:S(2)}) collective-permute-start(bf16[128,1024]{1,0:T(8,128)(2,1)S(1)} %get-tuple-element.91), channel_id=1, source_target_pairs={{0,32},{4,36},{8,40},{12,44},{16,48},{20,52},{24,56},{28,60},{32,6... | collective-permute-start | bytes 786440 | tf_op jit(solution)/shard_map/step3/ppermute | solution.py:33
  130.7 12.5 %collective-permute-start.19 = (bf16[192,1024]{1,0:T(8,128)(2,1)S(1)}, bf16[192,1024]{1,0:T(8,128)(2,1)S(1)}, u32[]{:S(2)}, u32[]{:S(2)}) collective-permute-start(bf16[192,1024]{1,0:T(8,128)(2,1)S(1)} %get-tuple-element.97), channel_id=1, source_target_pairs={{0,224},{4,228},{8,232},{12,236},{16,240},{20,244},{24,248},{28,25... | collective-permute-start | bytes 1179656 | tf_op jit(solution)/shard_map/step4/ppermute | solution.py:33
  135.2 11.1 %collective-permute-start.18 = (bf16[192,1024]{1,0:T(8,128)(2,1)S(1)}, bf16[192,1024]{1,0:T(8,128)(2,1)S(1)}, u32[]{:S(2)}, u32[]{:S(2)}) collective-permute-start(bf16[192,1024]{1,0:T(8,128)(2,1)S(1)} %get-tuple-element.95), channel_id=1, source_target_pairs={{0,32},{4,36},{8,40},{12,44},{16,48},{20,52},{24,56},{28,60},{32,6... | collective-permute-start | bytes 1179656 | tf_op jit(solution)/shard_map/step4/ppermute | solution.py:33
  135.2 8.1 %collective-permute-start.20 = (f32[4,1024]{1,0:T(4,128)S(1)}, f32[4,1024]{1,0:T(4,128)S(1)}, u32[]{:S(2)}, u32[]{:S(2)}) collective-permute-start(f32[4,1024]{1,0:T(4,128)S(1)} %add.90), channel_id=1, source_target_pairs={{0,32},{4,36},{8,40},{12,44},{16,48},{20,52},{24,56},{28,60},{32,0... | collective-permute-start | bytes 49160 | tf_op jit(solution)/shard_map/taps3/ppermute | solution.py:159
  155.8 8.0 %collective-permute-start.24 = (bf16[128,1024]{1,0:T(8,128)(2,1)S(1)}, bf16[128,1024]{1,0:T(8,128)(2,1)S(1)}, u32[]{:S(2)}, u32[]{:S(2)}) collective-permute-start(bf16[128,1024]{1,0:T(8,128)(2,1)S(1)} %get-tuple-element.104), channel_id=1, source_target_pairs={{0,32},{4,36},{8,40},{12,44},{16,48},{20,52},{24,56},{28,60},{32,6... | collective-permute-start | bytes 786440 | tf_op jit(solution)/shard_map/step6/ppermute | solution.py:33
  164.1 9.2 %collective-permute-start.26 = (bf16[128,1024]{1,0:T(8,128)(2,1)S(1)}, bf16[128,1024]{1,0:T(8,128)(2,1)S(1)}, u32[]{:S(2)}, u32[]{:S(2)}) collective-permute-start(bf16[128,1024]{1,0:T(8,128)(2,1)S(1)} %get-tuple-element.107), channel_id=1, source_target_pairs={{0,32},{4,36},{8,40},{12,44},{16,48},{20,52},{24,56},{28,60},{32,6... | collective-permute-start | bytes 786440 | tf_op jit(solution)/shard_map/step7/ppermute | solution.py:33
  (24 other events, 141.7 us)
